TPU v7x, 256 devices: a whole 4x4x8 slice. The times are simulated.
256 devices in a mesh: dz: 4 (over z_lo, core), dxy: 64 (over z_hi, y, x).
Axes of the slice: x: 4, y: 4, z: 8 (z_hi: 4, z_lo: 2; z = z_hi * 2 + z_lo), core: 2. Of those that a mesh axis runs over, the one named last changes fastest.
Arguments:
- queries: bfloat16 [32768, 1024], P(('dz', 'dxy')), may hold values from -180 to 180
- keys: bfloat16 [32768, 1024], P(('dz', 'dxy')), may hold values from -4 to 4
- values: bfloat16 [32768, 1024], P(('dz', 'dxy')), may hold values from -6 to 6
- out_grad: bfloat16 [32768, 1024], P(('dz', 'dxy')), may hold values from -24 to 24
- out_weight: bfloat16 [1024, 1024], replicated, may hold values from -0.1875 to 0.1875
- pair_counts: int32 [256, 9], P(('dz', 'dxy')), may hold values from 0 to 128, as said below
- counts: int32 [256], P(('dz', 'dxy')), may hold values from 2 to 128
Outputs:
- gradient_of_queries: bfloat16 [32768, 1024], P(('dz', 'dxy'))
- gradient_of_keys: bfloat16 [32768, 1024], P(('dz', 'dxy'))
- gradient_of_values: bfloat16 [32768, 1024], P(('dz', 'dxy'))
- wo_grad: float32 [1024, 1024], P('dxy')
Inputs may be any that keep to these rules, and one draw needn't show every extreme that they name: `pair_counts`: slot ((i + 1) * 3 + (j + 1)) + t of cell c refers to cell t of the domain at offset (i, j) from c's domain; its entry is that cell's entry of counts when the two cells are linked, else 0, and always 0 where the domain lies outside the grid. Links are symmetric and every cell is linked to itself.
All inputs are finite; a program needn't handle non-finite values.
Results may differ from a plain program's by a relative error of at most 0.02.
Values may be sent and summed in bfloat16 or wider, within the bound.
A program may use at most 128 MiB of HBM per device.

v0:
```python
import jax
import jax.numpy as jnp
from jax import lax
from jax.sharding import Mesh
from jax.sharding import PartitionSpec as P

HEADS = 16
CELL = 128
DZ_DXY = ("dz", "dxy_0", "dxy_1", "dxy_2")
DXY = ("dxy_0", "dxy_1", "dxy_2")


GROUP_HEADS = 4


def extended(block, sides, width):
    for axis, dim in sides:
        count = lax.axis_size(axis)
        forward = [(i, i + 1) for i in range(count - 1)]
        backward = [(target, source) for source, target in forward]
        low = lax.ppermute(
            lax.slice_in_dim(block, block.shape[dim] - width, None, axis=dim), axis, forward
        )
        high = lax.ppermute(lax.slice_in_dim(block, 0, width, axis=dim), axis, backward)
        block = jnp.concatenate([low, block, high], axis=dim)
    return block


def reduced_to_own(tiles, axes, order):
    lengths = [lax.axis_size(a) for a in axes]
    tiles = tiles.reshape(*lengths, *tiles.shape[1:])
    tiles = tiles.transpose(*order, *range(len(axes), tiles.ndim))
    tiles = tiles.reshape(-1, *tiles.shape[len(axes) :])
    for k in order:
        tiles = lax.psum_scatter(tiles, axes[k], scatter_dimension=0, tiled=True)
    return tiles[0]


def split_up(value, dim, count):
    lengths = value.shape
    tiles = value.reshape(*lengths[:dim], count, lengths[dim] // count, *lengths[dim + 1 :])
    return jnp.moveaxis(tiles, dim, 0)


def sum_by_axis(value, axes, order, dim):
    count = lax.axis_size(axes)
    return reduced_to_own(split_up(value, dim, count), axes, order)


def from_everyone(value, axis):
    count = lax.axis_size(axis)
    return lax.all_to_all(
        jnp.broadcast_to(value[None], (count, *value.shape)), axis, 0, 0, tiled=True
    )


def over_copies(value, axis):
    everything = from_everyone(value, axis)
    return jnp.sum(everything, axis=0)


def shards(queries, keys, values, out_grad, out_weight, pair_counts, counts):
    row_count, model_width = queries.shape
    head_width = model_width // HEADS
    logit_scale = head_width ** (-0.5)
    local_cells = counts.shape[0]
    key_rows = pair_counts.shape[1] * CELL
    group_width = GROUP_HEADS * head_width
    atom_index = jnp.arange(CELL, dtype=jnp.int32)
    live_rows = (atom_index[None, :] < counts[:, None]).reshape(row_count, 1)
    masked_grad = jnp.where(live_rows, out_grad, jnp.zeros_like(out_grad))
    out_delta = jnp.dot(masked_grad, out_weight, preferred_element_type=jnp.float32).astype(
        jnp.bfloat16
    )
    stacked = jnp.concatenate([keys, values], axis=1)[None, None]
    surround = extended(stacked, (("dz", 0), (DXY, 1)), 1)
    surround = surround.reshape(key_rows, 2 * model_width)
    adjacent_keys = surround[:, :model_width]
    adjacent_values = surround[:, model_width:]
    allowed = (atom_index[None, None, :] < pair_counts[:, :, None]).reshape(local_cells, key_rows)
    allowed = jnp.repeat(allowed, CELL, axis=0)[None]
    query_parts, attended_parts, lse_parts, delta_parts, near_key_parts, near_value_parts = (
        [],
        [],
        [],
        [],
        [],
        [],
    )
    for group_id in range(HEADS // GROUP_HEADS):
        columns = slice(group_id * group_width, (group_id + 1) * group_width)
        cluster_queries = queries[:, columns].reshape(row_count, GROUP_HEADS, head_width)
        cluster_delta = out_delta[:, columns].reshape(row_count, GROUP_HEADS, head_width)
        cluster_keys = adjacent_keys[:, columns].reshape(key_rows, GROUP_HEADS, head_width)
        cluster_values = adjacent_values[:, columns].reshape(key_rows, GROUP_HEADS, head_width)
        attention_logits = logit_scale * jnp.einsum(
            "qvy,pvy->vqp", cluster_queries, cluster_keys, preferred_element_type=jnp.float32
        )
        attention_logits = jnp.where(allowed, attention_logits, -1e30)
        highest = jnp.max(attention_logits, axis=-1, keepdims=True)
        weight_sum = jnp.sum(
            jnp.where(allowed, jnp.exp(attention_logits - highest), 0.0), axis=-1, keepdims=True
        )
        log_total = highest + jnp.log(weight_sum)
        probs = jnp.where(allowed, jnp.exp(attention_logits - log_total), 0.0)
        probabilities_reduced = probs.astype(jnp.bfloat16)
        attention_result = jnp.einsum(
            "gtl,lgs->tgs",
            probabilities_reduced,
            cluster_values,
            preferred_element_type=jnp.float32,
        ).astype(jnp.bfloat16)
        row_delta = jnp.sum(
            cluster_delta.astype(jnp.float32) * attention_result.astype(jnp.float32), axis=-1
        )
        probability_gradient = jnp.einsum(
            "qvy,pvy->vqp", cluster_delta, cluster_values, preferred_element_type=jnp.float32
        )
        score_gradient = (probs * (probability_gradient - row_delta.T[:, :, None])).astype(
            jnp.bfloat16
        )
        group_grad = logit_scale * jnp.einsum(
            "gtl,lgs->tgs", score_gradient, cluster_keys, preferred_element_type=jnp.float32
        )
        query_parts.append(group_grad.astype(jnp.bfloat16).reshape(row_count, group_width))
        attended_parts.append(attention_result.reshape(row_count, group_width))
        lse_parts.append(log_total[:, :, 0])
        delta_parts.append(row_delta.T)
    gradient_of_queries = jnp.concatenate(query_parts, axis=1)
    attended_all = jnp.concatenate(attended_parts, axis=1)
    paired = jnp.concatenate([queries, out_delta], axis=1)[None, None]
    near_pairs = extended(paired, (("dz", 0), (DXY, 1)), 1)
    near_pairs = near_pairs.reshape(key_rows, 2 * model_width)
    softmax_stats = jnp.stack(
        [jnp.concatenate(lse_parts, axis=0), jnp.concatenate(delta_parts, axis=0)]
    )
    softmax_stats = softmax_stats.reshape(1, 1, 2, HEADS * row_count)
    near_stats = extended(softmax_stats, (("dz", 0), (DXY, 1)), 1)
    near_stats = jnp.transpose(
        near_stats.reshape(3, 3, 2, HEADS, row_count), (2, 3, 0, 1, 4)
    ).reshape(2, HEADS, key_rows)
    linked = pair_counts > 0
    key_live = atom_index[None, :] < counts[:, None]
    owner_mask = linked.T[:, None, :, None] & key_live[None, None, :, :]
    owner_mask = jnp.broadcast_to(
        owner_mask, (pair_counts.shape[1], CELL, local_cells, CELL)
    ).reshape(key_rows, row_count)[None]
    key_parts, value_parts = ([], [])
    for group_id in range(HEADS // GROUP_HEADS):
        columns = slice(group_id * group_width, (group_id + 1) * group_width)
        heads_here = slice(group_id * GROUP_HEADS, (group_id + 1) * GROUP_HEADS)
        far_queries = near_pairs[:, :model_width][:, columns].reshape(
            key_rows, GROUP_HEADS, head_width
        )
        far_delta = near_pairs[:, model_width:][:, columns].reshape(
            key_rows, GROUP_HEADS, head_width
        )
        far_lse = near_stats[0, heads_here]
        far_rows = near_stats[1, heads_here]
        home_cell_keys = keys[:, columns].reshape(row_count, GROUP_HEADS, head_width)
        home_cell_values = values[:, columns].reshape(row_count, GROUP_HEADS, head_width)
        attention_logits = logit_scale * jnp.einsum(
            "sfc,nfc->fsn", far_queries, home_cell_keys, preferred_element_type=jnp.float32
        )
        probs = jnp.where(
            owner_mask,
            jnp.exp(jnp.where(owner_mask, attention_logits - far_lse[:, :, None], 0.0)),
            0.0,
        )
        probabilities_reduced = probs.astype(jnp.bfloat16)
        probability_gradient = jnp.einsum(
            "sfc,nfc->fsn", far_delta, home_cell_values, preferred_element_type=jnp.float32
        )
        score_gradient = (probs * (probability_gradient - far_rows[:, :, None])).astype(
            jnp.bfloat16
        )
        value_part = jnp.einsum(
            "ucy,cuo->yuo", probabilities_reduced, far_delta, preferred_element_type=jnp.float32
        )
        key_part = logit_scale * jnp.einsum(
            "ucy,cuo->yuo", score_gradient, far_queries, preferred_element_type=jnp.float32
        )
        key_parts.append(key_part.astype(jnp.bfloat16).reshape(row_count, group_width))
        value_parts.append(value_part.astype(jnp.bfloat16).reshape(row_count, group_width))
    gradient_of_keys = jnp.concatenate(key_parts, axis=1)
    gradient_of_values = jnp.concatenate(value_parts, axis=1)
    device_count = lax.axis_size("dz") * lax.axis_size(DXY)
    normalizer = (row_count * device_count) ** (-0.5)
    plane_rows = sum_by_axis(
        lax.dot_general(
            masked_grad, attended_all, (((0,), (0,)), ((), ())), preferred_element_type=jnp.float32
        ),
        DXY,
        (1, 2, 0),
        0,
    )
    wo_grad = over_copies(plane_rows, "dz") * normalizer
    return (gradient_of_queries, gradient_of_keys, gradient_of_values, wo_grad)


def solution(mesh):
    split = Mesh(mesh.devices.reshape(mesh.shape["dz"], 4, 4, 4), ("dz", "dxy_0", "dxy_1", "dxy_2"))
    return jax.shard_map(
        shards,
        mesh=split,
        in_specs=(
            P(DZ_DXY, None),
            P(DZ_DXY, None),
            P(DZ_DXY, None),
            P(DZ_DXY, None),
            P(),
            P(DZ_DXY, None),
            P(DZ_DXY),
        ),
        out_specs=(P(DZ_DXY, None), P(DZ_DXY, None), P(DZ_DXY, None), P(DXY, None)),
        check_vma=False,
    )
```

profile of v0, /device:TPU:31, one launch (start us, length us, event | category | flops | bytes accessed | tf_op | source)
XLA Modules:
  0.0 345.7 jit_solution(16966716261018256608)
XLA Ops:
  8.5 2.6 collective-permute-start.1
  11.0 3.4 collective-permute-start
  14.5 4.9 %collective-permute-done.1 = bf16[1,1,128,2048]{3,2,1,0:T(8,128)(2,1)S(1)} collective-permute-done((bf16[1,1,128,2048]{3,2,1,0:T(8,128)(2,1)S(1)}, bf16[1,1,128,2048]{3,2,1,0:T(8,128)(2,1)S(1)}, u32[]{:S(2)}, u32[]{:S(2)}) %collective-permute-start.1) | collective-permute-done | bytes 524320 | tf_op jit(solution)/shard_map/ppermute | solution.py:24
  24.5 7.9 %collective-permute-start.2 = (bf16[3,1,128,2048]{3,2,1,0:T(8,128)(2,1)}, bf16[3,1,128,2048]{3,2,1,0:T(8,128)(2,1)}, u32[]{:S(2)}, u32[]{:S(2)}) collective-permute-start(bf16[3,1,128,2048]{3,2,1,0:T(8,128)(2,1)} %pad_maximum_fusion.2), channel_id=1, source_target_pairs={{0,1},{1,2},{2,3},{3,4},{4,5},{5,6},{6,7},{7,8},{8,9},{9,10},{10,1... | collective-permute-start | bytes 4718600 | tf_op jit(solution)/shard_map/ppermute | solution.py:21
  40.4 53.7 %collective-permute-done.3 = bf16[3,1,128,2048]{3,2,1,0:T(8,128)(2,1)} collective-permute-done((bf16[3,1,128,2048]{3,2,1,0:T(8,128)(2,1)}, bf16[3,1,128,2048]{3,2,1,0:T(8,128)(2,1)}, u32[]{:S(2)}, u32[]{:S(2)}) %collective-permute-start.3) | collective-permute-done | bytes 1572896 | tf_op jit(solution)/shard_map/ppermute | solution.py:24
  126.1 4.9 %collective-permute-start.4 = (bf16[1,1,128,2048]{3,2,1,0:T(8,128)(2,1)S(1)}, bf16[1,1,128,2048]{3,2,1,0:T(8,128)(2,1)}, u32[]{:S(2)}, u32[]{:S(2)}) collective-permute-start(bf16[1,1,128,2048]{3,2,1,0:T(8,128)(2,1)S(1)} %maximum_bitcast_fusion.1), channel_id=1, source_target_pairs={{0,64},{64,128},{128,192},{1,65},{65,129},{129,193},{2,66},{66,130... | collective-permute-start | bytes 1572872 | tf_op jit(solution)/shard_map/ppermute | solution.py:21
  150.4 9.3 %collective-permute-start.6 = (bf16[3,1,128,2048]{3,2,1,0:T(8,128)(2,1)}, bf16[3,1,128,2048]{3,2,1,0:T(8,128)(2,1)}, u32[]{:S(2)}, u32[]{:S(2)}) collective-permute-start(bf16[3,1,128,2048]{3,2,1,0:T(8,128)(2,1)} %pad_maximum_fusion.3), channel_id=1, source_target_pairs={{0,1},{1,2},{2,3},{3,4},{4,5},{5,6},{6,7},{7,8},{8,9},{9,10},{10,1... | collective-permute-start | bytes 4718600 | tf_op jit(solution)/shard_map/ppermute | solution.py:21
  164.4 3.6 %collective-permute-start.8 = (f32[1,1,2,2048]{3,2,1,0:T(2,128)}, f32[1,1,2,2048]{3,2,1,0:T(2,128)}, u32[]{:S(2)}, u32[]{:S(2)}) collective-permute-start(f32[1,1,2,2048]{3,2,1,0:T(2,128)} %pad_maximum_fusion.9), channel_id=1, source_target_pairs={{0,64},{64,128},{128,192},{1,65},{65,129},{129,193},{2,66},{66,130... | collective-permute-start | bytes 49160 | tf_op jit(solution)/shard_map/ppermute | solution.py:21
  168.0 3.8 %fusion.112 = bf16[4,64,128]{2,1,0:T(8,128)(2,1)} fusion(bf16[1152,4,64]{0,2,1:T(8,128)(2,1)} %bitcast.213, bf16[128,4,64]{0,2,1:T(8,128)(2,1)} %bitcast.259, bf16[1152,4,64]{0,2,1:T(8,128)(2,1)} %bitcast.221, f32[4,128,1152]{1,2,0:T(8,128)} %copy-done.4, f32[4,128]{1,0:T(4,128)} %bitcast.276, f32[4,128]{1,0:T(4,128)} %copy-done.44, ...), kind=kOutput, calls=%fused_computation.137 | convolution fusion | flops 154009600 | bytes 3675264 | tf_op jit(solution)/shard_map/gtl,lgs->tgs/dot_general | solution.py:122
  171.9 3.8 %fusion.113 = bf16[4,64,128]{2,1,0:T(8,128)(2,1)} fusion(bf16[1152,4,64]{0,2,1:T(8,128)(2,1)} %bitcast.215, bf16[128,4,64]{0,2,1:T(8,128)(2,1)} %bitcast.263, bf16[1152,4,64]{0,2,1:T(8,128)(2,1)} %bitcast.223, f32[4,128,1152]{1,2,0:T(8,128)} %copy-done.5, f32[4,128]{1,0:T(4,128)S(1)} %bitcast.274, f32[4,128]{1,0:T(4,128)S(1)} %copy-done.41, ...), kind=kOutput, calls=%fused_computation.138 | convolution fusion | flops 154009600 | bytes 3675264 | tf_op jit(solution)/shard_map/gtl,lgs->tgs/dot_general | solution.py:122
  175.8 3.6 %fusion.114 = bf16[4,64,128]{2,1,0:T(8,128)(2,1)} fusion(bf16[1152,4,64]{0,2,1:T(8,128)(2,1)S(1)} %bitcast.212, bf16[128,4,64]{0,2,1:T(8,128)(2,1)} %bitcast.261, bf16[1152,4,64]{0,2,1:T(8,128)(2,1)} %bitcast.219, f32[4,128,1152]{1,2,0:T(8,128)} %copy-done.3, f32[4,128]{1,0:T(4,128)S(1)} %bitcast.272, f32[4,128]{1,0:T(4,128)S(1)} %copy-done.43, ...), kind=kOutput, calls=%fused_computation.139 | convolution fusion | flops 154009600 | bytes 3675264 | tf_op jit(solution)/shard_map/gtl,lgs->tgs/dot_general | solution.py:122
  179.4 45.2 %collective-permute-done.7 = bf16[3,1,128,2048]{3,2,1,0:T(8,128)(2,1)} collective-permute-done((bf16[3,1,128,2048]{3,2,1,0:T(8,128)(2,1)}, bf16[3,1,128,2048]{3,2,1,0:T(8,128)(2,1)}, u32[]{:S(2)}, u32[]{:S(2)}) %collective-permute-start.7) | collective-permute-done | bytes 1572896 | tf_op jit(solution)/shard_map/ppermute | solution.py:24
  229.0 3.0 fusion.115
  239.3 8.5 %collective-permute-start.10 = (f32[3,1,2,2048]{3,2,1,0:T(2,128)}, f32[3,1,2,2048]{3,2,1,0:T(2,128)}, u32[]{:S(2)}, u32[]{:S(2)}) collective-permute-start(f32[3,1,2,2048]{3,2,1,0:T(2,128)} %pad_maximum_fusion.8), channel_id=1, source_target_pairs={{0,1},{1,2},{2,3},{3,4},{4,5},{5,6},{6,7},{7,8},{8,9},{9,10},{10,1... | collective-permute-start | bytes 147464 | tf_op jit(solution)/shard_map/ppermute | solution.py:21
  260.9 3.0 fusion.108
  265.8 3.6 %fusion.25 = f32[4,1152,128]{2,1,0:T(8,128)} fusion(bf16[1152,4,64]{0,2,1:T(8,128)(2,1)} %bitcast.205, bf16[128,4,64]{0,2,1:T(8,128)(2,1)} %bitcast.262, f32[4,1152]{1,0:T(4,128)} %get-tuple-element.44, pred[1152,128]{1,0:T(8,128)(4,1)} %bitcast.243), kind=kOutput, calls=%fused_computation.43 | convolution fusion | flops 77856768 | bytes 3180544 | tf_op jit(solution)/shard_map/sfc,nfc->fsn/dot_general | solution.py:162
  269.4 3.7 %fusion.109 = bf16[4,64,128]{2,1,0:T(8,128)(2,1)} fusion(bf16[1152,4,64]{0,2,1:T(8,128)(2,1)} %bitcast.206, f32[4,1152,128]{2,1,0:T(8,128)} %fusion.25, bf16[1152,4,64]{0,2,1:T(8,128)(2,1)} %bitcast.197, bf16[128,4,64]{0,2,1:T(8,128)(2,1)} %bitcast.228, f32[4,1152]{1,0:T(4,128)} %get-tuple-element.43), kind=kOutput, calls=%fused_computation.134 | convolution fusion | flops 152829952 | bytes 3688448 | tf_op jit(solution)/shard_map/ucy,cuo->yuo/dot_general | solution.py:180
  274.7 3.6 %fusion.23 = f32[4,1152,128]{2,1,0:T(8,128)} fusion(bf16[1152,4,64]{0,2,1:T(8,128)(2,1)} %bitcast.203, bf16[128,4,64]{0,2,1:T(8,128)(2,1)} %bitcast.260, f32[4,1152]{1,0:T(4,128)} %get-tuple-element.46, pred[1152,128]{1,0:T(8,128)(4,1)} %bitcast.244), kind=kOutput, calls=%fused_computation.41 | convolution fusion | flops 77856768 | bytes 3180544 | tf_op jit(solution)/shard_map/sfc,nfc->fsn/dot_general | solution.py:162
  278.4 3.7 %fusion.110 = bf16[4,64,128]{2,1,0:T(8,128)(2,1)} fusion(bf16[1152,4,64]{0,2,1:T(8,128)(2,1)} %bitcast.204, f32[4,1152,128]{2,1,0:T(8,128)} %fusion.23, bf16[1152,4,64]{0,2,1:T(8,128)(2,1)S(1)} %bitcast.195, bf16[128,4,64]{0,2,1:T(8,128)(2,1)} %bitcast.227, f32[4,1152]{1,0:T(4,128)} %get-tuple-element.45), kind=kOutput, calls=%fused_computation.135 | convolution fusion | flops 152829952 | bytes 3688448 | tf_op jit(solution)/shard_map/ucy,cuo->yuo/dot_general | solution.py:180
  283.6 3.6 %fusion.21 = f32[4,1152,128]{2,1,0:T(8,128)} fusion(bf16[1152,4,64]{0,2,1:T(8,128)(2,1)} %bitcast.201, bf16[128,4,64]{0,2,1:T(8,128)(2,1)} %bitcast.258, f32[4,1152]{1,0:T(4,128)} %get-tuple-element.47, pred[1152,128]{1,0:T(8,128)(4,1)} %bitcast.245), kind=kOutput, calls=%fused_computation.39 | convolution fusion | flops 77856768 | bytes 3180544 | tf_op jit(solution)/shard_map/sfc,nfc->fsn/dot_general | solution.py:162
  287.2 3.7 %fusion.111 = bf16[4,64,128]{2,1,0:T(8,128)(2,1)} fusion(bf16[1152,4,64]{0,2,1:T(8,128)(2,1)} %bitcast.202, f32[4,1152,128]{2,1,0:T(8,128)} %fusion.21, bf16[1152,4,64]{0,2,1:T(8,128)(2,1)S(1)} %bitcast.193, bf16[128,4,64]{0,2,1:T(8,128)(2,1)} %bitcast.226, f32[4,1152]{1,0:T(4,128)} %get-tuple-element.40), kind=kOutput, calls=%fused_computation.136 | convolution fusion | flops 152829952 | bytes 3688448 | tf_op jit(solution)/shard_map/ucy,cuo->yuo/dot_general | solution.py:180
  296.3 2.8 fusion.122
  302.6 23.1 %reduce-scatter.8.cloned.1.call-done = f32[1,16,1024]{2,1,0:T(8,128)} async-done(((f32[4,16,1024]{2,1,0:T(8,128)}), f32[1,16,1024]{2,1,0:T(8,128)}) %reduce-scatter.8.cloned.1.call-update) | async-done | bytes 65552 | tf_op jit(solution)/shard_map/reduce_scatter | solution.py:35
  327.3 6.0 %all-to-all-start = ((f32[4,16,1024]{2,1,0:T(8,128)}), f32[4,16,1024]{2,1,0:T(8,128)S(1)}, u32[]{:S(2)}, u32[]{:S(2)}) async-start(f32[4,16,1024]{2,1,0:T(8,128)} %broadcast_in_dim.164), calls=%async_computation.3 | async-start | bytes 524288 | tf_op jit(solution)/shard_map/all_to_all | solution.py:52
  (220 shorter events, 115.0 us)
Async XLA Ops:
  7.2 258.3 %reduce-scatter.4.cloned.1.call-start = ((), (), s32[]{:S(2)}) async-start(), calls=%async_computation.4 | async-start | bytes 5242880 | tf_op jit(solution)/shard_map/reduce_scatter | solution.py:35
  8.5 11.0 %collective-permute-start.1 = (bf16[1,1,128,2048]{3,2,1,0:T(8,128)(2,1)S(1)}, bf16[1,1,128,2048]{3,2,1,0:T(8,128)(2,1)S(1)}, u32[]{:S(2)}, u32[]{:S(2)}) collective-permute-start(bf16[1,1,128,2048]{3,2,1,0:T(8,128)(2,1)S(1)} %maximum_bitcast_fusion), channel_id=1, source_target_pairs={{64,0},{128,64},{192,128},{65,1},{129,65},{193,129},{66,2},{130,66... | collective-permute-start | bytes 1572872 | tf_op jit(solution)/shard_map/ppermute | solution.py:24
  11.0 9.6 %collective-permute-start = (bf16[1,1,128,2048]{3,2,1,0:T(8,128)(2,1)S(1)}, bf16[1,1,128,2048]{3,2,1,0:T(8,128)(2,1)S(1)}, u32[]{:S(2)}, u32[]{:S(2)}) collective-permute-start(bf16[1,1,128,2048]{3,2,1,0:T(8,128)(2,1)S(1)} %maximum_bitcast_fusion), channel_id=1, source_target_pairs={{0,64},{64,128},{128,192},{1,65},{65,129},{129,193},{2,66},{66,130... | collective-permute-start | bytes 1572872 | tf_op jit(solution)/shard_map/ppermute | solution.py:21
  21.9 72.2 %collective-permute-start.3 = (bf16[3,1,128,2048]{3,2,1,0:T(8,128)(2,1)}, bf16[3,1,128,2048]{3,2,1,0:T(8,128)(2,1)}, u32[]{:S(2)}, u32[]{:S(2)}) collective-permute-start(bf16[3,1,128,2048]{3,2,1,0:T(8,128)(2,1)} %pad_maximum_fusion.2), channel_id=1, source_target_pairs={{1,0},{2,1},{3,2},{4,3},{5,4},{6,5},{7,6},{8,7},{9,8},{10,9},{11,1... | collective-permute-start | bytes 4718600 | tf_op jit(solution)/shard_map/ppermute | solution.py:24
  24.5 69.6 %collective-permute-start.2 = (bf16[3,1,128,2048]{3,2,1,0:T(8,128)(2,1)}, bf16[3,1,128,2048]{3,2,1,0:T(8,128)(2,1)}, u32[]{:S(2)}, u32[]{:S(2)}) collective-permute-start(bf16[3,1,128,2048]{3,2,1,0:T(8,128)(2,1)} %pad_maximum_fusion.2), channel_id=1, source_target_pairs={{0,1},{1,2},{2,3},{3,4},{4,5},{5,6},{6,7},{7,8},{8,9},{9,10},{10,1... | collective-permute-start | bytes 4718600 | tf_op jit(solution)/shard_map/ppermute | solution.py:21
  40.4 78.3 %copy-start.32 = (pred[1152]{0:T(1024)(128)(4,1)}, pred[1152]{0:T(1024)(128)(4,1)S(1)}, u32[]{:S(2)}) copy-start(pred[1152]{0:T(1024)(128)(4,1)S(1)} %bitcast_compare_fusion) | copy-start | bytes 3460
  114.9 45.5 %copy-start.40 = (f32[4,128]{1,0:T(4,128)}, f32[4,128]{1,0:T(4,128)S(1)}, u32[]{:S(2)}) copy-start(f32[4,128]{1,0:T(4,128)S(1)} %get-tuple-element.65) | copy-start | bytes 6148
  114.9 45.5 %copy-start.39 = (f32[4,128]{1,0:T(4,128)}, f32[4,128]{1,0:T(4,128)S(1)}, u32[]{:S(2)}) copy-start(f32[4,128]{1,0:T(4,128)S(1)} %get-tuple-element.67) | copy-start | bytes 6148
  123.0 173.2 %reduce-scatter.6.cloned.1.call-start = ((), (), s32[]{:S(2)}) async-start(), calls=%async_computation.5 | async-start | bytes 1310720 | tf_op jit(solution)/shard_map/reduce_scatter | solution.py:35
  124.2 21.7 %collective-permute-start.5 = (bf16[1,1,128,2048]{3,2,1,0:T(8,128)(2,1)S(1)}, bf16[1,1,128,2048]{3,2,1,0:T(8,128)(2,1)}, u32[]{:S(2)}, u32[]{:S(2)}) collective-permute-start(bf16[1,1,128,2048]{3,2,1,0:T(8,128)(2,1)S(1)} %maximum_bitcast_fusion.1), channel_id=1, source_target_pairs={{64,0},{128,64},{192,128},{65,1},{129,65},{193,129},{66,2},{130,66... | collective-permute-start | bytes 1572872 | tf_op jit(solution)/shard_map/ppermute | solution.py:24
  126.1 19.8 %collective-permute-start.4 = (bf16[1,1,128,2048]{3,2,1,0:T(8,128)(2,1)S(1)}, bf16[1,1,128,2048]{3,2,1,0:T(8,128)(2,1)}, u32[]{:S(2)}, u32[]{:S(2)}) collective-permute-start(bf16[1,1,128,2048]{3,2,1,0:T(8,128)(2,1)S(1)} %maximum_bitcast_fusion.1), channel_id=1, source_target_pairs={{0,64},{64,128},{128,192},{1,65},{65,129},{129,193},{2,66},{66,130... | collective-permute-start | bytes 1572872 | tf_op jit(solution)/shard_map/ppermute | solution.py:21
  148.5 76.1 %collective-permute-start.7 = (bf16[3,1,128,2048]{3,2,1,0:T(8,128)(2,1)}, bf16[3,1,128,2048]{3,2,1,0:T(8,128)(2,1)}, u32[]{:S(2)}, u32[]{:S(2)}) collective-permute-start(bf16[3,1,128,2048]{3,2,1,0:T(8,128)(2,1)} %pad_maximum_fusion.3), channel_id=1, source_target_pairs={{1,0},{2,1},{3,2},{4,3},{5,4},{6,5},{7,6},{8,7},{9,8},{10,9},{11,1... | collective-permute-start | bytes 4718600 | tf_op jit(solution)/shard_map/ppermute | solution.py:24
  150.4 74.2 %collective-permute-start.6 = (bf16[3,1,128,2048]{3,2,1,0:T(8,128)(2,1)}, bf16[3,1,128,2048]{3,2,1,0:T(8,128)(2,1)}, u32[]{:S(2)}, u32[]{:S(2)}) collective-permute-start(bf16[3,1,128,2048]{3,2,1,0:T(8,128)(2,1)} %pad_maximum_fusion.3), channel_id=1, source_target_pairs={{0,1},{1,2},{2,3},{3,4},{4,5},{5,6},{6,7},{7,8},{8,9},{9,10},{10,1... | collective-permute-start | bytes 4718600 | tf_op jit(solution)/shard_map/ppermute | solution.py:21
  162.5 73.5 %collective-permute-start.9 = (f32[1,1,2,2048]{3,2,1,0:T(2,128)}, f32[1,1,2,2048]{3,2,1,0:T(2,128)}, u32[]{:S(2)}, u32[]{:S(2)}) collective-permute-start(f32[1,1,2,2048]{3,2,1,0:T(2,128)} %pad_maximum_fusion.9), channel_id=1, source_target_pairs={{64,0},{128,64},{192,128},{65,1},{129,65},{193,129},{66,2},{130,66... | collective-permute-start | bytes 49160 | tf_op jit(solution)/shard_map/ppermute | solution.py:24
  164.4 71.6 %collective-permute-start.8 = (f32[1,1,2,2048]{3,2,1,0:T(2,128)}, f32[1,1,2,2048]{3,2,1,0:T(2,128)}, u32[]{:S(2)}, u32[]{:S(2)}) collective-permute-start(f32[1,1,2,2048]{3,2,1,0:T(2,128)} %pad_maximum_fusion.9), channel_id=1, source_target_pairs={{0,64},{64,128},{128,192},{1,65},{65,129},{129,193},{2,66},{66,130... | collective-permute-start | bytes 49160 | tf_op jit(solution)/shard_map/ppermute | solution.py:21
  237.4 19.3 %collective-permute-start.11 = (f32[3,1,2,2048]{3,2,1,0:T(2,128)}, f32[3,1,2,2048]{3,2,1,0:T(2,128)}, u32[]{:S(2)}, u32[]{:S(2)}) collective-permute-start(f32[3,1,2,2048]{3,2,1,0:T(2,128)} %pad_maximum_fusion.8), channel_id=1, source_target_pairs={{1,0},{2,1},{3,2},{4,3},{5,4},{6,5},{7,6},{8,7},{9,8},{10,9},{11,1... | collective-permute-start | bytes 147464 | tf_op jit(solution)/shard_map/ppermute | solution.py:24
  239.3 17.4 %collective-permute-start.10 = (f32[3,1,2,2048]{3,2,1,0:T(2,128)}, f32[3,1,2,2048]{3,2,1,0:T(2,128)}, u32[]{:S(2)}, u32[]{:S(2)}) collective-permute-start(f32[3,1,2,2048]{3,2,1,0:T(2,128)} %pad_maximum_fusion.8), channel_id=1, source_target_pairs={{0,1},{1,2},{2,3},{3,4},{4,5},{5,6},{6,7},{7,8},{8,9},{9,10},{10,1... | collective-permute-start | bytes 147464 | tf_op jit(solution)/shard_map/ppermute | solution.py:21
  265.5 60.2 %reduce-scatter.8.cloned.1.call-start = ((), (), s32[]{:S(2)}) async-start(), calls=%async_computation.6 | async-start | bytes 327680 | tf_op jit(solution)/shard_map/reduce_scatter | solution.py:35
  301.6 34.0 %copy-start.26 = (bf16[128,256]{1,0:T(8,128)(2,1)S(1)}, bf16[128,256]{1,0:T(8,128)(2,1)}, u32[]{:S(2)}) copy-start(bf16[128,256]{1,0:T(8,128)(2,1)} %copy.222) | copy-start | bytes 196612
  301.6 34.0 %copy-start.27 = (bf16[128,256]{1,0:T(8,128)(2,1)S(1)}, bf16[128,256]{1,0:T(8,128)(2,1)}, u32[]{:S(2)}) copy-start(bf16[128,256]{1,0:T(8,128)(2,1)} %copy.221) | copy-start | bytes 196612
  301.6 34.0 %copy-start.28 = (bf16[128,256]{1,0:T(8,128)(2,1)S(1)}, bf16[128,256]{1,0:T(8,128)(2,1)}, u32[]{:S(2)}) copy-start(bf16[128,256]{1,0:T(8,128)(2,1)} %copy.220) | copy-start | bytes 196612
  301.6 34.8 %copy-start.29 = (bf16[128,256]{1,0:T(8,128)(2,1)S(1)}, bf16[128,256]{1,0:T(8,128)(2,1)}, u32[]{:S(2)}) copy-start(bf16[128,256]{1,0:T(8,128)(2,1)} %copy.227) | copy-start | bytes 196612
  301.6 34.8 %copy-start.30 = (bf16[128,256]{1,0:T(8,128)(2,1)S(1)}, bf16[128,256]{1,0:T(8,128)(2,1)}, u32[]{:S(2)}) copy-start(bf16[128,256]{1,0:T(8,128)(2,1)} %copy.226) | copy-start | bytes 196612
  327.3 11.2 %all-to-all-start = ((f32[4,16,1024]{2,1,0:T(8,128)}), f32[4,16,1024]{2,1,0:T(8,128)S(1)}, u32[]{:S(2)}, u32[]{:S(2)}) async-start(f32[4,16,1024]{2,1,0:T(8,128)} %broadcast_in_dim.164), calls=%async_computation.3 | async-start | bytes 524288 | tf_op jit(solution)/shard_map/all_to_all | solution.py:52
  (43 other events, 317.8 us)
Sparse Core Ops, SparseCore 0:
  123.1 64.4 reduce-scatter.3
  265.7 28.5 reduce-scatter.5
  296.8 28.9 reduce-scatter.7
where the time goes:
time: 349 us; the launch traced here: 346 us
  waiting for transfers between devices  130 us (37%)
  local copies, waits for them, and re-layouts  62.5 us (18%)
  matrix products  60.6 us (17%)
  starting transfers between devices  56.9 us (16%)
  other arithmetic  20.9 us (6%)
  between operations  15.1 us (4%)
    ppermute x6, waiting for transfers between devices, extended(): lax.ppermute(lax.slice_in_dim(block, 0, width, axis=dim), axis, backward)  104 us
    ppermute x6, starting transfers between devices, extended(): lax.ppermute(lax.slice_in_dim(block, block.shape[dim] - width, None, axis...  37.7 us
    reduce_scatter x3, waiting for transfers between devices, reduced_to_own(): tiles = lax.psum_scatter(tiles, axes[k], scatter_dimension=0, tiled=True)  23.1 us
    unnamed x114, local copies, waits for them, and re-layouts  17.1 us
    dot_general x4, matrix products, shards(): jnp.einsum('gtl,lgs->tgs', score_gradient, cluster_keys, preferred_elemen...  14.4 us
    dot_general x4, matrix products, shards(): jnp.einsum('ucy,cuo->yuo', score_gradient, far_queries, preferred_element...  14.2 us
    dot_general x4, matrix products, shards(): jnp.einsum('sfc,nfc->fsn', far_queries, home_cell_keys, preferred_element...  13 us
    ppermute x6, starting transfers between devices, extended(): lax.ppermute(lax.slice_in_dim(block, 0, width, axis=dim), axis, backward)  12.8 us
  transfers between devices with their start and end apart: 16, of which 6 were waited for; matrix products, arithmetic and copies ran while one was open for 32% of the time, Pallas kernels for 0%

commit v1 on v0

v1 whole, which is shorter than its diff:
```python
import jax
import jax.numpy as jnp
from jax import lax
from jax.experimental import pallas as pl
from jax.experimental.pallas import tpu as pltpu
from jax.sharding import PartitionSpec as P

MESH = pl.DeviceIdType.MESH
BF = jnp.bfloat16
F32 = jnp.float32
CELL = 128
GW = 256
DOWN, UP = 0, 1
K_, V_, Q_, G_, C_ = 0, 1, 2, 3, 4
NEG = -1e30


def dot(a, b):
    return jnp.dot(a, b, preferred_element_type=F32)


def halves_t(x):
    row = lax.broadcasted_iota(jnp.int32, x.shape, 0)
    zero = jnp.zeros_like(x)
    return jnp.concatenate(
        [jnp.where(row < 64, x, zero), jnp.where(row < 64, zero, x)], axis=1
    )


def halves(x):
    lane = lax.broadcasted_iota(jnp.int32, x.shape, 1)
    zero = jnp.zeros_like(x)
    return jnp.concatenate(
        [jnp.where(lane < 64, x, zero), jnp.where(lane < 64, zero, x)], axis=0
    )


def diagonal(x):
    return jnp.concatenate([x[:64, :128], x[64:, 128:]], axis=0)


def kernel(
    q_hbm, k_hbm, v_hbm, g_hbm, w_hbm, pair_ref, count_ref,
    dq_hbm, dk_hbm, dv_hbm, wo_ref,
    kv, kvt, qs, gm, graw, gown, ww, do, pc, pcs,
    sbuf, pbuf, dsb, dos, delta, att, acc, dqs,
    hold, back, got, hold2, fin, wsum, wgot, x2, xgot,
    loc, a_s, a_r, b_s, b_r, l_s, l_r, d_s, d_r, m_s, m_r, f_s, f_r, u_s, u_r, x_s, x_r,
):
    me = lax.axis_index("dz")
    p = lax.axis_index("dxy")
    low = me < 2
    sib = me + 1 - 2 * (me % 2)
    zpeer = (me + 2) % 4
    places = 64

    def logical(layer, at):
        return jnp.where(at < 2, layer, 3 - layer)

    def layer_of(ll):
        return jnp.where(low, ll, 3 - ll)

    mine = logical(me, me)

    has = {DOWN: p > 0, UP: p < places - 1}
    gets = {DOWN: p < places - 1, UP: p > 0}
    step = {DOWN: -1, UP: 1}
    cross = {
        DOWN: (p % 16 == 0) & (p > 0),
        UP: (p % 16 == 15) & (p < places - 1),
    }
    via = {DOWN: p + 15, UP: p - 15}
    relays = {
        DOWN: (p % 16 == 15) & (p >= 16),
        UP: (p % 16 == 0) & (p < places - 16),
    }
    relay_from = {DOWN: p - 15, UP: p + 15}
    relay_to = {DOWN: p - 16, UP: p + 16}
    crossed = {DOWN: (p % 16 == 15) & (p < places - 1), UP: (p % 16 == 0) & (p > 0)}
    crossed_via = {DOWN: p + 16, UP: p - 16}
    side = {DOWN: 2, UP: 0}

    def cl(x):
        return jnp.clip(x, 0, places - 1)

    def rows(ll, j):
        return pl.ds(pl.multiple_of((ll * 3 + j) * CELL, CELL), CELL)

    def cols(t):
        return pl.ds(pl.multiple_of(t * GW, GW), GW)

    def cell(ll):
        return pl.ds(pl.multiple_of(ll * CELL, CELL), CELL)

    def remote(src, dst, ss, rs, dz, place):
        return pltpu.make_async_remote_copy(
            src_ref=src, dst_ref=dst, send_sem=ss, recv_sem=rs,
            device_id=(dz, place), device_id_type=MESH,
        )

    own = cols(me)
    loads = [
        pltpu.make_async_copy(k_hbm.at[:, own], kv.at[0, rows(mine, 1)], loc.at[0]),
        pltpu.make_async_copy(v_hbm.at[:, own], kv.at[1, rows(mine, 1)], loc.at[1]),
        pltpu.make_async_copy(q_hbm.at[:, own], qs.at[cell(mine)], loc.at[2]),
        pltpu.make_async_copy(g_hbm, graw, loc.at[3]),
        pltpu.make_async_copy(w_hbm.at[:, own], ww, loc.at[4]),
    ]
    for c in loads:
        c.start()

    u, x = p // 4, p % 4
    peers = []
    for e in range(1, 16):
        peers.append((None, me, ((u + e) % 16) * 4 + x))
    at = me * 4 + x
    for e in range(1, 16):
        to = (at + e) % 16
        peers.append((None, to // 4, u * 4 + to % 4))
    for d in (DOWN, UP):
        peers.append((has[d], me, cl(p + step[d])))
        peers.append((cross[d], me, cl(via[d])))
        peers.append((relays[d], me, cl(relay_from[d])))
        peers.append((relays[d], me, cl(relay_to[d])))
        peers.append((crossed[d], me, cl(crossed_via[d])))
    barrier = pltpu.get_barrier_semaphore()
    expect = 0
    for ok, a, b in peers:

        def greet(a=a, b=b):
            pl.semaphore_signal(barrier, inc=1, device_id=(a, b), device_id_type=MESH)

        if ok is None:
            greet()
            expect = expect + 1
        else:
            pl.when(ok)(greet)
            expect = expect + jnp.where(ok, 1, 0)

    lane = lax.broadcasted_iota(jnp.int32, (8, 128), 1)
    plain = jnp.zeros((8, 128), jnp.int32)
    turned = jnp.zeros((8, 128), jnp.int32)
    for s in range(9):
        plain = jnp.where(lane == s, pair_ref[0, s], plain)
        turned = jnp.where(lane == (2 - s // 3) * 3 + s % 3, pair_ref[0, s], turned)
    pcs[0] = plain
    pcs[1] = turned
    pc[mine] = jnp.where(low, plain, turned)

    def clear(d):
        for ll in range(4):
            kv[:, (ll * 3 + side[d]) * CELL : (ll * 3 + side[d] + 1) * CELL, :] = (
                jnp.zeros((2, CELL, GW), BF)
            )
            got[d, ll] = jnp.zeros((2, CELL, GW), BF)

    for d in (DOWN, UP):
        pl.when(jnp.logical_not(gets[d]))(lambda d=d: clear(d))

    pl.semaphore_wait(barrier, expect)

    def spread(kind, o):
        t = (me + o) % 4
        lt = logical(me, t)
        if kind == C_:
            turn = jnp.where(t < 2, 0, 1)
            return remote(pcs.at[turn], pc.at[lt], a_s.at[C_, o], a_r.at[C_, lt], t, p)
        src = (k_hbm, v_hbm, q_hbm)[kind].at[:, cols(t)]
        dst = kv.at[kind, rows(lt, 1)] if kind != Q_ else qs.at[cell(lt)]
        return remote(src, dst, a_s.at[kind, o], a_r.at[kind, lt], t, p)

    def arrived(kind, ll):
        if kind == C_:
            dst = pc.at[ll]
        elif kind == G_:
            dst = gm.at[cell(ll)]
        elif kind == Q_:
            dst = qs.at[cell(ll)]
        else:
            dst = kv.at[kind, rows(ll, 1)]
        remote(dst, dst, a_s.at[kind, 0], a_r.at[kind, ll], sib, p).wait_recv()

    for kind in (K_, V_):
        for o in (1, 3, 2):
            spread(kind, o).start()

    def halo(d, ll, kind, place=None):
        blk = kv.at[kind, rows(ll, 1)]
        dst = kv.at[kind, rows(ll, side[d])]
        return remote(
            blk, dst, b_s.at[d, ll, kind], b_r.at[d, ll, kind], me, cl(p + step[d])
        )

    def halo_detour(d, ll):
        blk = kv.at[1, rows(ll, 1)]
        return remote(
            blk, hold.at[d, ll], b_s.at[d, ll, 1], l_r.at[d, ll], me, cl(via[d])
        )

    def halo_forward(d, ll):
        dst = kv.at[1, rows(ll, side[d])]
        return remote(
            hold.at[d, ll], dst, l_s.at[d, ll], b_r.at[d, ll, 1], me, cl(relay_to[d])
        )

    def send_halo(ll, kind):
        for d in (UP, DOWN):
            if kind == 0:
                pl.when(has[d])(lambda d=d: halo(d, ll, 0).start())
            else:
                pl.when(has[d] & jnp.logical_not(cross[d]))(
                    lambda d=d: halo(d, ll, 1).start()
                )
                pl.when(cross[d])(lambda d=d: halo_detour(d, ll).start())

    def forward_halo(ll):
        for d in (UP, DOWN):

            def go(d=d):
                halo_detour(d, ll).wait_recv()
                halo_forward(d, ll).start()

            pl.when(relays[d])(go)

    loads[0].wait()
    send_halo(mine, 0)
    loads[1].wait()
    send_halo(mine, 1)
    other = 1 - mine
    for kind in (0, 1):
        arrived(kind, other)
        send_halo(other, kind)

    for kind in (Q_, C_):
        for o in (3, 2, 1):
            spread(kind, o).start()

    loads[3].wait()
    live = lax.broadcasted_iota(jnp.int32, (CELL, 1024), 0) < count_ref[0]
    gown[...] = jnp.where(live, graw[...], jnp.zeros((CELL, 1024), BF))
    own_g = pltpu.make_async_copy(gown, gm.at[cell(mine)], loc.at[5])
    own_g.start()

    def g_to(t, o):
        lt = logical(me, t)
        return remote(gown, gm.at[cell(lt)], a_s.at[G_, o], a_r.at[G_, lt], t, p)

    zl = logical(zpeer, me)
    g_sib = g_to(sib, 1)
    g_z = g_to(zpeer, 2)
    g_fwd = remote(
        gm.at[cell(zl)], gm.at[cell(zl)], a_s.at[G_, 3], a_r.at[G_, zl], sib, p
    )
    g_z.start()
    g_sib.start()

    for ll in (2, 3):
        for kind in (0, 1):
            arrived(kind, ll)
            send_halo(ll, kind)

    arrived(G_, zl)
    g_fwd.start()

    forward_halo(0)
    forward_halo(1)
    forward_halo(2)
    forward_halo(3)

    loads[4].wait()
    own_g.wait()
    arrived(G_, other)
    arrived(G_, 5 - zl)
    for ll in range(4):
        do[cell(ll)] = dot(gm[cell(ll)], ww[...]).astype(BF)

    loads[2].wait()
    for kind in (Q_, C_):
        arrived(kind, other)
        arrived(kind, 2)
        arrived(kind, 3)
    for ll in range(4):
        qs[cell(ll)] = qs[cell(ll)] * jnp.asarray(0.125, BF)

    def halo_arrived(ll):
        for d in (UP, DOWN):
            for kind in (0, 1):
                pl.when(gets[d])(lambda d=d, kind=kind: halo(d, ll, kind).wait_recv())

    def turn_layer(ll):
        for j in range(3):
            for kind in (0, 1):
                at_ = (ll * 3 + j) * CELL
                kvt[kind, :, at_ : at_ + CELL] = kv[kind, at_ : at_ + CELL, :].T

    first = [0, 0, 1, 2]
    last = [1, 2, 3, 3]
    base = [0, 768, 1920, 3072]
    sub = lax.broadcasted_iota(jnp.int32, (CELL, 128), 0)

    def fold(op, v):
        return op(v.reshape(CELL // 8, 8, 256), axis=0)

    def forward(lq):
        bias = jnp.where(sub < pc[lq][0:1, :], 0.0, NEG)
        slots = [(ll, j) for ll in range(first[lq], last[lq] + 1) for j in range(3)]
        n = len(slots) * CELL
        r0 = first[lq] * 3 * CELL
        cq = slice(lq * CELL, (lq + 1) * CELL)
        for hp in range(2):
            hc = slice(hp * 128, hp * 128 + 128)
            qt = halves_t(qs[cq, hc].T)
            top = None
            for i, (ll, j) in enumerate(slots):
                at_ = (ll * 3 + j) * CELL
                k9 = (ll - lq + 1) * 3 + j
                s = dot(kv[0, at_ : at_ + CELL, hc], qt) + bias[:, k9 : k9 + 1]
                sbuf[i * CELL : (i + 1) * CELL, :] = s
                t = fold(jnp.max, s)
                top = t if top is None else jnp.maximum(top, t)
            top = jnp.max(top, axis=0, keepdims=True)
            total = None
            b0 = base[lq]
            for i in range(len(slots)):
                e = jnp.exp(sbuf[i * CELL : (i + 1) * CELL, :] - top)
                pbuf[hp, b0 + i * CELL : b0 + (i + 1) * CELL, :] = e.astype(BF)
                t = fold(jnp.sum, e)
                total = t if total is None else total + t
            inv = 1.0 / jnp.sum(total, axis=0, keepdims=True)
            at_t = dot(kvt[1, hc, r0 : r0 + n], pbuf[hp, b0 : b0 + n, :])
            at_t = diagonal(at_t * inv).astype(BF)
            att[cq, hc] = at_t.T
            inv2 = jnp.concatenate(
                [
                    jnp.broadcast_to(inv[:, :128], (64, 128)),
                    jnp.broadcast_to(inv[:, 128:], (64, 128)),
                ],
                axis=0,
            )
            dt = (do[cq, hc].T.astype(F32) * inv2).astype(BF)
            dos[lq, hp] = dt
            prod = dt.astype(F32) * at_t.astype(F32)
            dl = jnp.concatenate(
                [
                    jnp.sum(prod[:64], axis=0, keepdims=True),
                    jnp.sum(prod[64:], axis=0, keepdims=True),
                ],
                axis=1,
            )
            delta[lq, hp] = jnp.broadcast_to(dl, (8, 256))

    def backward(lq):
        slots = [(ll, j) for ll in range(first[lq], last[lq] + 1) for j in range(3)]
        n = len(slots) * CELL
        r0 = first[lq] * 3 * CELL
        cq = slice(lq * CELL, (lq + 1) * CELL)
        b0 = base[lq]
        for hp in range(2):
            hc = slice(hp * 128, hp * 128 + 128)
            dt = dos[lq, hp]
            dmt = halves_t(dt)
            dm = halves(dt.T)
            qm = halves(qs[cq, hc])
            dl = delta[lq, hp][0:1, :]
            for i, (ll, j) in enumerate(slots):
                at_ = (ll * 3 + j) * CELL
                pr = pbuf[hp, b0 + i * CELL : b0 + (i + 1) * CELL, :]
                dp = dot(kv[1, at_ : at_ + CELL, hc], dmt)
                ds = (pr.astype(F32) * (dp - dl)).astype(BF)
                dsb[i * CELL : (i + 1) * CELL, :] = ds
                dv = dot(pr, dm)
                dk = dot(ds, qm)
                if lq == max(ll - 1, 0):
                    acc[1, at_ : at_ + CELL, hc] = dv
                    acc[0, at_ : at_ + CELL, hc] = dk
                else:
                    acc[1, at_ : at_ + CELL, hc] += dv
                    acc[0, at_ : at_ + CELL, hc] += dk
            dqt = dot(kvt[0, hc, r0 : r0 + n], dsb[0:n, :])
            dqs[cq, hc] = (diagonal(dqt) * 0.125).T.astype(BF)

    def part(d, ll, kind):
        return remote(
            back.at[d, ll, kind], got.at[d, ll, kind],
            d_s.at[d, ll, kind], d_r.at[d, ll, kind], me, cl(p + step[d]),
        )

    def part_detour(d, ll):
        return remote(
            back.at[d, ll, 1], hold2.at[d, ll],
            d_s.at[d, ll, 1], m_r.at[d, ll], me, cl(via[d]),
        )

    def part_forward(d, ll):
        return remote(
            hold2.at[d, ll], got.at[d, ll, 1],
            m_s.at[d, ll], d_r.at[d, ll, 1], me, cl(relay_to[d]),
        )

    def send_parts(ll):
        for d in (UP, DOWN):
            j = 2 if d == UP else 0
            at_ = (ll * 3 + j) * CELL
            for kind in (1, 0):
                back[d, ll, kind] = acc[kind, at_ : at_ + CELL, :].astype(BF)

            def near(d=d):
                part(d, ll, 1).start()

            def detour(d=d):
                part_detour(d, ll).start()

            def keys(d=d):
                part(d, ll, 0).start()

            pl.when(has[d] & jnp.logical_not(cross[d]))(near)
            pl.when(cross[d])(detour)
            pl.when(has[d])(keys)

    def forward_parts(ll):
        for d in (UP, DOWN):

            def go(d=d):
                part_detour(d, ll).wait_recv()
                part_forward(d, ll).start()

            pl.when(relays[d])(go)

    def home(kind, ll, src):
        t = layer_of(ll)
        out = (dk_hbm, dv_hbm, dq_hbm)[kind].at[:, cols(me)]
        o = (t - me + 4) % 4
        far = remote(src, out, f_s.at[kind, ll], f_r.at[kind, o], t, p)
        near = pltpu.make_async_copy(src, out, f_s.at[kind, ll])
        return far, near

    def send_home(kind, ll, src):
        far, near = home(kind, ll, src)
        if ll >= 2:
            far.start()
        else:
            pl.when(mine != ll)(lambda: far.start())
            pl.when(mine == ll)(lambda: near.start())

    def sent_home(kind, ll, src):
        far, near = home(kind, ll, src)
        if ll >= 2:
            far.wait_send()
        else:
            pl.when(mine != ll)(lambda: far.wait_send())
            pl.when(mine == ll)(lambda: near.wait())

    def finish(ll):
        for d in (UP, DOWN):
            for kind in (0, 1):
                pl.when(gets[d])(lambda d=d, kind=kind: part(d, ll, kind).wait_recv())
        at_ = (ll * 3 + 1) * CELL
        for kind in (0, 1):
            s = acc[kind, at_ : at_ + CELL, :]
            s = s + got[0, ll, kind].astype(F32) + got[1, ll, kind].astype(F32)
            fin[kind, ll] = s.astype(BF)
            send_home(kind, ll, fin.at[kind, ll])

    halo_arrived(0)
    turn_layer(0)
    halo_arrived(1)
    turn_layer(1)
    forward(0)
    backward(0)
    send_home(2, 0, dqs.at[cell(0)])
    halo_arrived(2)
    turn_layer(2)
    forward(1)
    backward(1)
    send_home(2, 1, dqs.at[cell(1)])
    send_parts(0)
    halo_arrived(3)
    turn_layer(3)
    forward(2)
    forward(3)

    wsum[...] = lax.dot_general(
        gm[...], att[...], (((0,), (0,)), ((), ())), preferred_element_type=F32
    ).astype(BF)

    def stage1(e):
        to = (u + e) % 16
        return remote(
            wsum.at[pl.ds(pl.multiple_of(to * 64, 64), 64)], wgot.at[e],
            u_s.at[e], u_r.at[e], me, to * 4 + x,
        )

    for e in range(1, 16):
        stage1(e).start()
    forward_parts(0)
    backward(2)
    send_home(2, 2, dqs.at[cell(2)])
    send_parts(1)
    backward(3)
    send_home(2, 3, dqs.at[cell(3)])
    send_parts(2)
    send_parts(3)
    forward_parts(1)
    forward_parts(2)
    forward_parts(3)

    mine_w = wsum[pl.ds(pl.multiple_of(u * 64, 64), 64), :].astype(F32)
    for e in range(1, 16):
        stage1(e).wait_recv()
        mine_w = mine_w + wgot[e].astype(F32)
    x2[...] = mine_w

    def stage2(e):
        to = (at + e) % 16
        return remote(
            x2.at[pl.ds(pl.multiple_of((to % 4) * 16, 16), 16)],
            xgot.at[x, :, cols(me)],
            x_s.at[e], x_r.at[e], to // 4, u * 4 + to % 4,
        )

    for e in range(1, 16):
        stage2(e).start()
    own_x = pltpu.make_async_copy(
        x2.at[pl.ds(pl.multiple_of(x * 16, 16), 16)], xgot.at[x, :, cols(me)], loc.at[6]
    )
    own_x.start()

    finish(0)
    finish(1)
    finish(2)
    finish(3)

    own_x.wait()
    for e in range(1, 16):
        came = (at - e + 16) % 16
        spot = xgot.at[came % 4, :, cols(came // 4)]
        remote(spot, spot, x_s.at[e], x_r.at[e], sib, p).wait_recv()
    wo_ref[...] = (xgot[0] + xgot[1] + xgot[2] + xgot[3]) * (32768 ** -0.5)

    for kind in range(3):
        for o in range(1, 4):
            spot = (dk_hbm, dv_hbm, dq_hbm)[kind].at[:, cols((me - o + 4) % 4)]
            remote(spot, spot, f_s.at[kind, 0], f_r.at[kind, o], sib, p).wait_recv()
    for ll in range(4):
        sent_home(0, ll, fin.at[0, ll])
        sent_home(1, ll, fin.at[1, ll])
        sent_home(2, ll, dqs.at[cell(ll)])
    for kind in (K_, V_, Q_, C_):
        for o in (1, 2, 3):
            spread(kind, o).wait_send()
    g_sib.wait_send()
    g_z.wait_send()
    g_fwd.wait_send()
    for e in range(1, 16):
        stage1(e).wait_send()
        stage2(e).wait_send()
    for ll in range(4):
        for d in (UP, DOWN):

            def sent(d=d):
                halo(d, ll, 0).wait_send()
                halo(d, ll, 1).wait_send()
                part(d, ll, 0).wait_send()
                part(d, ll, 1).wait_send()

            def relayed(d=d):
                halo_forward(d, ll).wait_send()
                part_forward(d, ll).wait_send()

            pl.when(has[d])(sent)
            pl.when(relays[d])(relayed)


def shards(queries, keys, values, out_grad, out_weight, pair_counts, counts):
    n, width = queries.shape
    big = pl.BlockSpec(memory_space=pl.ANY)
    small = pl.BlockSpec(memory_space=pltpu.SMEM)
    dma = pltpu.SemaphoreType.DMA
    wide = jax.ShapeDtypeStruct((n, width), BF)
    return pl.pallas_call(
        kernel,
        name="cell_attention_backward",
        out_shape=(wide, wide, wide, jax.ShapeDtypeStruct((16, width), F32)),
        in_specs=[big] * 5 + [small] * 2,
        out_specs=(big, big, big, pl.BlockSpec(memory_space=pltpu.VMEM)),
        scratch_shapes=[
            pltpu.VMEM((2, 1536, GW), BF),
            pltpu.VMEM((2, GW, 1536), BF),
            pltpu.VMEM((512, GW), BF),
            pltpu.VMEM((512, 1024), BF),
            pltpu.VMEM((CELL, 1024), BF),
            pltpu.VMEM((CELL, 1024), BF),
            pltpu.VMEM((1024, GW), BF),
            pltpu.VMEM((512, GW), BF),
            pltpu.VMEM((4, 8, 128), jnp.int32),
            pltpu.VMEM((2, 8, 128), jnp.int32),
            pltpu.VMEM((1152, 256), F32),
            pltpu.VMEM((2, 3840, 256), BF),
            pltpu.VMEM((1152, 256), BF),
            pltpu.VMEM((4, 2, 128, 128), BF),
            pltpu.VMEM((4, 2, 8, 256), F32),
            pltpu.VMEM((512, GW), BF),
            pltpu.VMEM((2, 1536, GW), F32),
            pltpu.VMEM((512, GW), BF),
            pltpu.VMEM((2, 4, CELL, GW), BF),
            pltpu.VMEM((2, 4, 2, CELL, GW), BF),
            pltpu.VMEM((2, 4, 2, CELL, GW), BF),
            pltpu.VMEM((2, 4, CELL, GW), BF),
            pltpu.VMEM((2, 4, CELL, GW), BF),
            pltpu.VMEM((1024, GW), BF),
            pltpu.VMEM((16, 64, GW), BF),
            pltpu.VMEM((64, GW), F32),
            pltpu.VMEM((4, 16, 1024), F32),
            dma((7,)),
            dma((5, 4)),
            dma((5, 4)),
            dma((2, 4, 2)),
            dma((2, 4, 2)),
            dma((2, 4)),
            dma((2, 4)),
            dma((2, 4, 2)),
            dma((2, 4, 2)),
            dma((2, 4)),
            dma((2, 4)),
            dma((3, 4)),
            dma((3, 4)),
            dma((16,)),
            dma((16,)),
            dma((16,)),
            dma((16,)),
        ],
        compiler_params=pltpu.CompilerParams(
            collective_id=0, has_side_effects=True, vmem_limit_bytes=48 * 2**20
        ),
        cost_estimate=pl.CostEstimate(
            flops=3_000_000_000, bytes_accessed=4_000_000, transcendentals=2_000_000
        ),
    )(queries, keys, values, out_grad, out_weight, pair_counts, counts)


def solution(mesh):
    both = P(("dz", "dxy"), None)
    return jax.shard_map(
        shards,
        mesh=mesh,
        in_specs=(both, both, both, both, P(), both, P(("dz", "dxy"))),
        out_specs=(both, both, both, P("dxy", None)),
        check_vma=False,
    )
```

time: 349 us -> 89.6 us (0.26)
  the two profiles are of different devices: /device:TPU:31 before, /device:TPU:97 now
where the time goes in v1:
time: 89.6 us; the launch traced here: 89.4 us
  Pallas kernels  79.3 us (89%)
  local copies, waits for them, and re-layouts  8.78 us (10%)
  between operations  1.3 us (1%)
    pallas_call x1, Pallas kernels, shards(): pl.pallas_call(kernel, name='cell_attention_backward', out_shape=(wide, w...  79.3 us
    unnamed x16, local copies, waits for them, and re-layouts  8.78 us

profile of v1, /device:TPU:97, one launch (start us, length us, event | category | flops | bytes accessed | tf_op | source)
XLA Modules:
  0.0 89.4 jit_solution(13794351765617902214)
XLA Ops:
  1.3 0.0 copy-start
  1.3 1.6 %copy-done = bf16[1024,1024]{1,0:T(8,128)(2,1)S(1)} copy-done((bf16[1024,1024]{1,0:T(8,128)(2,1)S(1)}, bf16[1024,1024]{1,0:T(8,128)(2,1)}, u32[]{:S(2)}) %copy-start) | copy-done | bytes 2097176
  2.9 0.0 copy-start.1
  2.9 0.9 %copy-done.1 = bf16[128,1024]{1,0:T(8,128)(2,1)S(1)} copy-done((bf16[128,1024]{1,0:T(8,128)(2,1)S(1)}, bf16[128,1024]{1,0:T(8,128)(2,1)}, u32[]{:S(2)}) %copy-start.1) | copy-done | bytes 262168
  3.8 0.0 copy-start.2
  3.8 0.9 %copy-done.2 = bf16[128,1024]{1,0:T(8,128)(2,1)S(1)} copy-done((bf16[128,1024]{1,0:T(8,128)(2,1)S(1)}, bf16[128,1024]{1,0:T(8,128)(2,1)}, u32[]{:S(2)}) %copy-start.2) | copy-done | bytes 262168
  4.8 0.0 copy-start.3
  4.8 0.9 %copy-done.3 = bf16[128,1024]{1,0:T(8,128)(2,1)S(1)} copy-done((bf16[128,1024]{1,0:T(8,128)(2,1)S(1)}, bf16[128,1024]{1,0:T(8,128)(2,1)}, u32[]{:S(2)}) %copy-start.3) | copy-done | bytes 262168
  5.7 0.0 copy-start.4
  5.7 0.9 %copy-done.4 = bf16[128,1024]{1,0:T(8,128)(2,1)S(1)} copy-done((bf16[128,1024]{1,0:T(8,128)(2,1)S(1)}, bf16[128,1024]{1,0:T(8,128)(2,1)}, u32[]{:S(2)}) %copy-start.4) | copy-done | bytes 262168
  6.7 0.0 copy-start.5
  6.7 0.7 copy-done.5
  7.3 79.3 %cell_attention_backward.1 = (bf16[128,1024]{1,0:T(8,128)(2,1)S(1)}, bf16[128,1024]{1,0:T(8,128)(2,1)S(1)}, bf16[128,1024]{1,0:T(8,128)(2,1)S(1)}, f32[16,1024]{1,0:T(8,128)S(1)}) custom-call(bf16[128,1024]{1,0:T(8,128)(2,1)S(1)} %copy-done.1, bf16[128,1024]{1,0:T(8,128)(2,1)S(1)} %copy-done.2, bf16[128,1024]{1,0:T(8,128)(2,1)S(1)} %copy-done.3, ...), custom_call_target="tpu_custom_call" | custom-call | flops 3000000000 | bytes 4000000 | tf_op jit(solution)/shard_map/cell_attention_backward/pallas_call | solution.py:580
  86.6 0.7 copy.16
  87.3 0.7 copy.17
  88.0 0.7 copy.18
  88.7 0.6 copy.19
Async XLA Ops:
  1.3 1.6 %copy-start = (bf16[1024,1024]{1,0:T(8,128)(2,1)S(1)}, bf16[1024,1024]{1,0:T(8,128)(2,1)}, u32[]{:S(2)}) copy-start(bf16[1024,1024]{1,0:T(8,128)(2,1)} %w_hbm.1) | copy-start | bytes 6291460
  2.9 0.9 %copy-start.1 = (bf16[128,1024]{1,0:T(8,128)(2,1)S(1)}, bf16[128,1024]{1,0:T(8,128)(2,1)}, u32[]{:S(2)}) copy-start(bf16[128,1024]{1,0:T(8,128)(2,1)} %q_hbm.1) | copy-start | bytes 786436
  3.8 0.9 %copy-start.2 = (bf16[128,1024]{1,0:T(8,128)(2,1)S(1)}, bf16[128,1024]{1,0:T(8,128)(2,1)}, u32[]{:S(2)}) copy-start(bf16[128,1024]{1,0:T(8,128)(2,1)} %k_hbm.1) | copy-start | bytes 786436
  4.8 0.9 %copy-start.3 = (bf16[128,1024]{1,0:T(8,128)(2,1)S(1)}, bf16[128,1024]{1,0:T(8,128)(2,1)}, u32[]{:S(2)}) copy-start(bf16[128,1024]{1,0:T(8,128)(2,1)} %v_hbm.1) | copy-start | bytes 786436
  5.7 0.9 %copy-start.4 = (bf16[128,1024]{1,0:T(8,128)(2,1)S(1)}, bf16[128,1024]{1,0:T(8,128)(2,1)}, u32[]{:S(2)}) copy-start(bf16[128,1024]{1,0:T(8,128)(2,1)} %g_hbm.1) | copy-start | bytes 786436
  6.7 0.7 copy-start.5

commit v2 on v1

v2 whole, which is shorter than its diff:
```python
import jax
import jax.numpy as jnp
from jax import lax
from jax.experimental import pallas as pl
from jax.experimental.pallas import tpu as pltpu
from jax.sharding import PartitionSpec as P

MESH = pl.DeviceIdType.MESH
BF = jnp.bfloat16
F32 = jnp.float32
CELL = 128
GW = 256
DOWN, UP = 0, 1
K_, V_, Q_, D_, G_, C_ = 0, 1, 2, 3, 4, 5
WAY = {(0, 0): 1, (0, 1): 2, (1, 0): 3, (1, 1): 0, (2, 0): 1, (2, 1): 2, (3, 0): 3, (3, 1): 0}
VIA = {1: -15, 2: -3, 3: -12}
ONTO = {1: 16, 2: 4, 3: 13}
NEG = -1e30


def dot(a, b):
    return jnp.dot(a, b, preferred_element_type=F32)


def halves_t(x):
    row = lax.broadcasted_iota(jnp.int32, x.shape, 0)
    zero = jnp.zeros_like(x)
    return jnp.concatenate(
        [jnp.where(row < 64, x, zero), jnp.where(row < 64, zero, x)], axis=1
    )


def halves(x):
    lane = lax.broadcasted_iota(jnp.int32, x.shape, 1)
    zero = jnp.zeros_like(x)
    return jnp.concatenate(
        [jnp.where(lane < 64, x, zero), jnp.where(lane < 64, zero, x)], axis=0
    )


def diagonal(x):
    return jnp.concatenate([x[:64, :128], x[64:, 128:]], axis=0)


def kernel(
    q_hbm, k_hbm, v_hbm, g_hbm, w_hbm, pair_ref, count_ref,
    dq_hbm, dk_hbm, dv_hbm, wo_ref,
    kv, kvt, qs, gm, graw, gown, ww, dhome, do, pc, pcs,
    sbuf, pbuf, dsb, scale, att, acc, dqs,
    hold, back, got, hold2, fin, wsum, wgot, w2, w2got, w3, w3got,
    loc, a_s, a_r, b_s, b_r, l_s, l_r, d_s, d_r, m_s, m_r, f_s, f_r, u_s, u_r, x_s, x_r, y_s, y_r,
):
    me = lax.axis_index("dz")
    p = lax.axis_index("dxy")
    low = me < 2
    sib = me + 1 - 2 * (me % 2)
    zpeer = (me + 2) % 4
    zdiag = (sib + 2) % 4
    group = (sib, zpeer, zdiag)
    places = 64

    def logical(layer, at):
        return jnp.where(at < 2, layer, 3 - layer)

    def layer_of(ll):
        return jnp.where(low, ll, 3 - ll)

    mine = logical(me, me)

    has = {DOWN: p > 0, UP: p < places - 1}
    gets = {DOWN: p < places - 1, UP: p > 0}
    step = {DOWN: -1, UP: 1}
    cross = {
        DOWN: (p % 16 == 0) & (p > 0),
        UP: (p % 16 == 15) & (p < places - 1),
    }
    crossed = {DOWN: (p % 16 == 15) & (p < places - 1), UP: (p % 16 == 0) & (p > 0)}
    relays = {}
    for r in (1, 2, 3):
        relays[UP, r] = (p % 16 == (15 + VIA[r]) % 16) & (p - VIA[r] < places - 1)
        relays[DOWN, r] = (p % 16 == -VIA[r] % 16) & (p + VIA[r] > 0)

    def via(d, r):
        return cl(p + step[d] * VIA[r])

    def relay_from(d, r):
        return cl(p - step[d] * VIA[r])

    def relay_to(d, r):
        return cl(p + step[d] * ONTO[r])

    def crossed_via(d, r):
        return cl(p - step[d] * ONTO[r])

    side = {DOWN: 2, UP: 0}

    def cl(x):
        return jnp.clip(x, 0, places - 1)

    def rows(ll, j):
        return pl.ds(pl.multiple_of((ll * 3 + j) * CELL, CELL), CELL)

    def cols(t):
        return pl.ds(pl.multiple_of(t * GW, GW), GW)

    def cell(ll):
        return pl.ds(pl.multiple_of(ll * CELL, CELL), CELL)

    def remote(src, dst, ss, rs, dz, place):
        return pltpu.make_async_remote_copy(
            src_ref=src, dst_ref=dst, send_sem=ss, recv_sem=rs,
            device_id=(dz, place), device_id_type=MESH,
        )

    own = cols(me)
    loads = [
        pltpu.make_async_copy(k_hbm.at[:, own], kv.at[0, rows(mine, 1)], loc.at[0]),
        pltpu.make_async_copy(v_hbm.at[:, own], kv.at[1, rows(mine, 1)], loc.at[1]),
        pltpu.make_async_copy(q_hbm.at[:, own], qs.at[cell(mine)], loc.at[2]),
        pltpu.make_async_copy(g_hbm, graw, loc.at[3]),
        pltpu.make_async_copy(w_hbm, ww, loc.at[4]),
    ]
    for c in loads:
        c.start()

    zh, y, x = p // 16, (p // 4) % 4, p % 4
    at = zh * 4 + me

    def in_column(e):
        return zh * 16 + ((y + e) % 4) * 4 + x

    def in_row(e):
        return zh * 16 + y * 4 + (x + e) % 4

    def across(e):
        to = (at + e) % 16
        return to % 4, (to // 4) * 16 + y * 4 + x

    peers = []
    for e in range(1, 4):
        peers.append((None, me, in_column(e)))
        peers.append((None, me, in_row(e)))
    for e in range(1, 16):
        peers.append((None, *across(e)))
    for d in (DOWN, UP):
        peers.append((has[d], me, cl(p + step[d])))
        for r in (1, 2, 3):
            peers.append((cross[d], me, via(d, r)))
            peers.append((relays[d, r], me, relay_from(d, r)))
            peers.append((relays[d, r], me, relay_to(d, r)))
            peers.append((crossed[d], me, crossed_via(d, r)))
    barrier = pltpu.get_barrier_semaphore()
    expect = 0
    for ok, a, b in peers:

        def greet(a=a, b=b):
            pl.semaphore_signal(barrier, inc=1, device_id=(a, b), device_id_type=MESH)

        if ok is None:
            greet()
            expect = expect + 1
        else:
            pl.when(ok)(greet)
            expect = expect + jnp.where(ok, 1, 0)

    lane = lax.broadcasted_iota(jnp.int32, (8, 128), 1)
    plain = jnp.zeros((8, 128), jnp.int32)
    turned = jnp.zeros((8, 128), jnp.int32)
    for s in range(9):
        plain = jnp.where(lane == s, pair_ref[0, s], plain)
        turned = jnp.where(lane == (2 - s // 3) * 3 + s % 3, pair_ref[0, s], turned)
    pcs[0] = plain
    pcs[1] = turned
    pc[mine] = jnp.where(low, plain, turned)

    def clear(d):
        for ll in range(4):
            kv[:, (ll * 3 + side[d]) * CELL : (ll * 3 + side[d] + 1) * CELL, :] = (
                jnp.zeros((2, CELL, GW), BF)
            )
            got[d, ll] = jnp.zeros((2, CELL, GW), BF)

    for d in (DOWN, UP):
        pl.when(jnp.logical_not(gets[d]))(lambda d=d: clear(d))

    pl.semaphore_wait(barrier, expect)

    def landing(kind, ll):
        if kind == C_:
            return pc.at[ll]
        if kind in (K_, V_):
            return kv.at[kind, rows(ll, 1)]
        return {Q_: qs, D_: do, G_: gm}[kind].at[cell(ll)]

    def spread(kind, i):
        t = group[i]
        lt = logical(me, t)
        if kind == C_:
            src = pcs.at[jnp.where(t < 2, 0, 1)]
        elif kind == G_:
            src = gown
        else:
            src = {K_: k_hbm, V_: v_hbm, Q_: q_hbm, D_: dhome}[kind].at[:, cols(t)]
        return remote(
            src, landing(kind, lt), a_s.at[kind, i], a_r.at[kind, lt], t, p
        )

    def arrived(kind, ll):
        dst = landing(kind, ll)
        remote(dst, dst, a_s.at[kind, 0], a_r.at[kind, ll], sib, p).wait_recv()

    for kind in (K_, V_, C_, Q_):
        for i in range(3):
            spread(kind, i).start()

    def halo(d, ll, kind):
        blk = kv.at[kind, rows(ll, 1)]
        dst = kv.at[kind, rows(ll, side[d])]
        return remote(
            blk, dst, b_s.at[d, ll, kind], b_r.at[d, ll, kind], me, cl(p + step[d])
        )

    def halo_detour(d, ll, kind, r):
        blk = kv.at[kind, rows(ll, 1)]
        return remote(
            blk, hold.at[d, ll], b_s.at[d, ll, kind], l_r.at[d, ll], me, via(d, r)
        )

    def halo_forward(d, ll, kind, r):
        dst = kv.at[kind, rows(ll, side[d])]
        return remote(
            hold.at[d, ll], dst, l_s.at[d, ll], b_r.at[d, ll, kind], me, relay_to(d, r)
        )

    def part(d, ll, kind):
        return remote(
            back.at[d, ll, kind], got.at[d, ll, kind],
            d_s.at[d, ll, kind], d_r.at[d, ll, kind], me, cl(p + step[d]),
        )

    def part_detour(d, ll, kind, r):
        return remote(
            back.at[d, ll, kind], hold2.at[d, ll],
            d_s.at[d, ll, kind], m_r.at[d, ll], me, via(d, r),
        )

    def part_forward(d, ll, kind, r):
        return remote(
            hold2.at[d, ll], got.at[d, ll, kind],
            m_s.at[d, ll], d_r.at[d, ll, kind], me, relay_to(d, r),
        )

    def send_beside(pos, ll, kind, straight, detour):
        r = WAY[pos, kind]
        for d in (UP, DOWN):
            if r == 0:
                pl.when(has[d])(lambda d=d: straight(d, ll, kind).start())
            else:
                pl.when(has[d] & jnp.logical_not(cross[d]))(
                    lambda d=d: straight(d, ll, kind).start()
                )
                pl.when(cross[d])(lambda d=d: detour(d, ll, kind, r).start())

    def pass_on(pos, ll, detour, forward):
        for kind in (0, 1):
            r = WAY[pos, kind]
            if r == 0:
                continue
            for d in (UP, DOWN):

                def go(d=d):
                    detour(d, ll, kind, r).wait_recv()
                    forward(d, ll, kind, r).start()

                pl.when(relays[d, r])(go)

    def send_halo(pos, ll, kind):
        send_beside(pos, ll, kind, halo, halo_detour)

    def forward_halo(pos, ll):
        pass_on(pos, ll, halo_detour, halo_forward)

    other = 1 - mine
    loads[0].wait()
    send_halo(0, mine, 0)
    loads[1].wait()
    send_halo(0, mine, 1)
    for kind in (0, 1):
        arrived(kind, other)
        send_halo(1, other, kind)

    loads[3].wait()
    live = lax.broadcasted_iota(jnp.int32, (CELL, 1024), 0) < count_ref[0]
    gown[...] = jnp.where(live, graw[...], jnp.zeros((CELL, 1024), BF))
    own_g = pltpu.make_async_copy(gown, gm.at[cell(mine)], loc.at[5])
    own_g.start()
    spread(G_, 1).start()
    spread(G_, 0).start()
    loads[4].wait()
    for c in range(4):
        dhome[:, c * GW : (c + 1) * GW] = dot(
            gown[...], ww[:, c * GW : (c + 1) * GW]
        ).astype(BF)
    own_d = pltpu.make_async_copy(dhome.at[:, own], do.at[cell(mine)], loc.at[6])
    own_d.start()
    spread(D_, 0).start()

    forward_halo(0, mine)
    forward_halo(1, other)
    for kind in (0, 1):
        for ll in (2, 3):
            arrived(kind, ll)
            send_halo(ll, ll, kind)
    zl = logical(zpeer, me)
    g_fwd = remote(
        gm.at[cell(zl)], gm.at[cell(zl)], a_s.at[G_, 2], a_r.at[G_, zl], sib, p
    )

    def halo_arrived(ll):
        for d in (UP, DOWN):
            for kind in (0, 1):
                pl.when(gets[d])(lambda d=d, kind=kind: halo(d, ll, kind).wait_recv())

    def turn_layer(ll):
        for j in range(3):
            for kind in (0, 1):
                at_ = (ll * 3 + j) * CELL
                kvt[kind, :, at_ : at_ + CELL] = kv[kind, at_ : at_ + CELL, :].T

    first = [0, 0, 1, 2]
    last = [1, 2, 3, 3]
    base = [0, 768, 1920, 3072]
    sub = lax.broadcasted_iota(jnp.int32, (CELL, 128), 0)

    def fold(op, v):
        return op(v.reshape(CELL // 8, 8, 256), axis=0)

    def forward(lq):
        bias = jnp.where(sub < pc[lq][0:1, :], 0.0, NEG)
        slots = [(ll, j) for ll in range(first[lq], last[lq] + 1) for j in range(3)]
        n = len(slots) * CELL
        r0 = first[lq] * 3 * CELL
        cq = slice(lq * CELL, (lq + 1) * CELL)
        for hp in range(2):
            hc = slice(hp * 128, hp * 128 + 128)
            qt = halves_t((qs[cq, hc] * jnp.asarray(0.125, BF)).T)
            top = None
            for i, (ll, j) in enumerate(slots):
                at_ = (ll * 3 + j) * CELL
                k9 = (ll - lq + 1) * 3 + j
                s = dot(kv[0, at_ : at_ + CELL, hc], qt) + bias[:, k9 : k9 + 1]
                sbuf[i * CELL : (i + 1) * CELL, :] = s
                t = fold(jnp.max, s)
                top = t if top is None else jnp.maximum(top, t)
            top = jnp.max(top, axis=0, keepdims=True)
            total = None
            b0 = base[lq]
            for i in range(len(slots)):
                e = jnp.exp(sbuf[i * CELL : (i + 1) * CELL, :] - top)
                pbuf[hp, b0 + i * CELL : b0 + (i + 1) * CELL, :] = e.astype(BF)
                t = fold(jnp.sum, e)
                total = t if total is None else total + t
            inv = 1.0 / jnp.sum(total, axis=0, keepdims=True)
            at_t = dot(kvt[1, hc, r0 : r0 + n], pbuf[hp, b0 : b0 + n, :])
            att[hc, cq] = diagonal(at_t * inv).astype(BF)
            scale[lq, hp] = jnp.broadcast_to(inv, (8, 256))

    def backward(lq):
        slots = [(ll, j) for ll in range(first[lq], last[lq] + 1) for j in range(3)]
        n = len(slots) * CELL
        r0 = first[lq] * 3 * CELL
        cq = slice(lq * CELL, (lq + 1) * CELL)
        b0 = base[lq]
        for hp in range(2):
            hc = slice(hp * 128, hp * 128 + 128)
            inv = scale[lq, hp][0:1, :]
            inv = jnp.concatenate(
                [
                    jnp.broadcast_to(inv[:, :128], (64, 128)),
                    jnp.broadcast_to(inv[:, 128:], (64, 128)),
                ],
                axis=0,
            )
            dt = (do[cq, hc].T.astype(F32) * inv).astype(BF)
            prod = dt.astype(F32) * att[hc, cq].astype(F32)
            dl = jnp.concatenate(
                [
                    jnp.sum(prod[:64], axis=0, keepdims=True),
                    jnp.sum(prod[64:], axis=0, keepdims=True),
                ],
                axis=1,
            )
            dmt = halves_t(dt)
            dm = halves(dt.T)
            qm = halves(qs[cq, hc] * jnp.asarray(0.125, BF))
            for i, (ll, j) in enumerate(slots):
                at_ = (ll * 3 + j) * CELL
                pr = pbuf[hp, b0 + i * CELL : b0 + (i + 1) * CELL, :]
                dp = dot(kv[1, at_ : at_ + CELL, hc], dmt)
                ds = (pr.astype(F32) * (dp - dl)).astype(BF)
                dsb[i * CELL : (i + 1) * CELL, :] = ds
                dv = dot(pr, dm)
                dk = dot(ds, qm)
                if lq == max(ll - 1, 0):
                    acc[1, at_ : at_ + CELL, hc] = dv
                    acc[0, at_ : at_ + CELL, hc] = dk
                else:
                    acc[1, at_ : at_ + CELL, hc] += dv
                    acc[0, at_ : at_ + CELL, hc] += dk
            dqt = dot(kvt[0, hc, r0 : r0 + n], dsb[0:n, :])
            dqs[cq, hc] = (diagonal(dqt) * 0.125).T.astype(BF)

    def send_parts(ll):
        for d in (UP, DOWN):
            j = 2 if d == UP else 0
            at_ = (ll * 3 + j) * CELL
            for kind in (1, 0):
                back[d, ll, kind] = acc[kind, at_ : at_ + CELL, :].astype(BF)
        for kind in (1, 0):
            send_beside(ll, ll, kind, part, part_detour)

    def forward_parts(ll):
        pass_on(ll, ll, part_detour, part_forward)

    def home(kind, ll, src):
        t = layer_of(ll)
        out = (dk_hbm, dv_hbm, dq_hbm)[kind].at[:, cols(me)]
        o = (t - me + 4) % 4
        return remote(src, out, f_s.at[kind, ll], f_r.at[kind, o], t, p)

    def keep(kind, ll, src):
        out = (dk_hbm, dv_hbm, dq_hbm)[kind].at[:, cols(me)]
        return pltpu.make_async_copy(src, out, f_s.at[kind, ll])

    def send_home(kind, ll, src):
        if ll >= 2:
            home(kind, ll, src).start()
        else:
            pl.when(mine != ll)(lambda: home(kind, ll, src).start())
            pl.when(mine == ll)(lambda: keep(kind, ll, src).start())

    def sent_home(kind, ll, src):
        if ll >= 2:
            home(kind, ll, src).wait_send()
        else:
            pl.when(mine != ll)(lambda: home(kind, ll, src).wait_send())
            pl.when(mine == ll)(lambda: keep(kind, ll, src).wait())

    def finish(ll):
        for d in (UP, DOWN):
            for kind in (0, 1):
                pl.when(gets[d])(lambda d=d, kind=kind: part(d, ll, kind).wait_recv())
        at_ = (ll * 3 + 1) * CELL
        for kind in (0, 1):
            s = acc[kind, at_ : at_ + CELL, :]
            s = s + got[0, ll, kind].astype(F32) + got[1, ll, kind].astype(F32)
            fin[kind, ll] = s.astype(BF)
            send_home(kind, ll, fin.at[kind, ll])

    def stage1(e):
        return remote(
            wsum.at[:, (y + e) % 4], wgot.at[e], u_s.at[e], u_r.at[e], me, in_column(e)
        )

    def stage2(e):
        return remote(
            w2.at[:, (x + e) % 4], w2got.at[e], y_s.at[e], y_r.at[e], me, in_row(e)
        )

    def stage3(e):
        t, place = across(e)
        to = (at + e) % 16
        return remote(
            w3.at[to // 4], w3got.at[zh, :, cols(me)], x_s.at[e], x_r.at[e], t, place
        )

    loads[2].wait()
    own_d.wait()
    for kind in (C_, Q_, D_):
        arrived(kind, other)
    halo_arrived(0)
    turn_layer(0)
    halo_arrived(1)
    turn_layer(1)
    forward(0)
    spread(D_, 1).start()
    spread(D_, 2).start()
    forward_halo(2, 2)
    forward_halo(3, 3)
    backward(0)
    send_home(2, 0, dqs.at[cell(0)])
    halo_arrived(2)
    turn_layer(2)
    forward(1)
    backward(1)
    send_parts(0)
    send_home(2, 1, dqs.at[cell(1)])
    for kind in (C_, Q_):
        arrived(kind, 2)
        arrived(kind, 3)
    halo_arrived(3)
    turn_layer(3)
    forward(2)
    arrived(G_, zl)
    g_fwd.start()
    forward(3)
    own_g.wait()
    arrived(G_, other)
    arrived(G_, 5 - zl)
    for i in range(4):
        w_t = dot(att[...], gm[:, i * 256 : (i + 1) * 256]).astype(BF)
        wsum[i] = w_t.T.reshape(4, 64, GW)
    for e in range(1, 4):
        stage1(e).start()
    arrived(D_, 2)
    arrived(D_, 3)
    backward(2)
    send_parts(1)
    send_home(2, 2, dqs.at[cell(2)])
    forward_parts(0)
    backward(3)
    send_parts(2)
    send_parts(3)
    send_home(2, 3, dqs.at[cell(3)])
    finish(0)

    s1 = wsum[:, y].astype(F32)
    for e in range(1, 4):
        stage1(e).wait_recv()
        s1 = s1 + wgot[e].astype(F32)
    w2[...] = s1.astype(BF).reshape(4, 4, 16, GW)
    for e in range(1, 4):
        stage2(e).start()
    forward_parts(1)
    finish(1)
    forward_parts(2)

    s2 = w2[:, x].astype(F32)
    for e in range(1, 4):
        stage2(e).wait_recv()
        s2 = s2 + w2got[e].astype(F32)
    w3[...] = s2.astype(BF)
    for e in range(1, 16):
        stage3(e).start()
    own_x = pltpu.make_async_copy(w3.at[zh], w3got.at[zh, :, cols(me)], loc.at[7])
    own_x.start()
    forward_parts(3)
    finish(2)
    finish(3)
    own_x.wait()
    for e in range(1, 16):
        came = (at - e + 16) % 16
        spot = w3got.at[came // 4, :, cols(came % 4)]
        remote(spot, spot, x_s.at[e], x_r.at[e], sib, p).wait_recv()
    total = w3got[0].astype(F32)
    for i in range(1, 4):
        total = total + w3got[i].astype(F32)
    wo_ref[...] = total * (32768**-0.5)

    for kind in range(3):
        for o in range(1, 4):
            spot = (dk_hbm, dv_hbm, dq_hbm)[kind].at[:, cols((me - o + 4) % 4)]
            remote(spot, spot, f_s.at[kind, 0], f_r.at[kind, o], sib, p).wait_recv()
    for ll in range(4):
        sent_home(0, ll, fin.at[0, ll])
        sent_home(1, ll, fin.at[1, ll])
        sent_home(2, ll, dqs.at[cell(ll)])
    for kind in (K_, V_, Q_, D_, C_):
        for i in range(3):
            spread(kind, i).wait_send()
    spread(G_, 0).wait_send()
    spread(G_, 1).wait_send()
    g_fwd.wait_send()
    for e in range(1, 4):
        stage1(e).wait_send()
        stage2(e).wait_send()
    for e in range(1, 16):
        stage3(e).wait_send()
    for d in (UP, DOWN):

        def sent(d=d):
            for ll in range(4):
                for kind in (0, 1):
                    halo(d, ll, kind).wait_send()
                    part(d, ll, kind).wait_send()

        pl.when(has[d])(sent)
        for pos, ll in enumerate((mine, other, 2, 3)):
            for kind in (0, 1):
                r = WAY[pos, kind]
                if r:
                    pl.when(relays[d, r])(
                        lambda d=d: halo_forward(d, ll, kind, r).wait_send()
                    )
                r = WAY[pos, kind]
                if r:
                    pl.when(relays[d, r])(
                        lambda d=d: part_forward(d, pos, kind, r).wait_send()
                    )


def shards(queries, keys, values, out_grad, out_weight, pair_counts, counts):
    n, width = queries.shape
    big = pl.BlockSpec(memory_space=pltpu.HBM)
    small = pl.BlockSpec(memory_space=pltpu.SMEM)
    dma = pltpu.SemaphoreType.DMA
    wide = jax.ShapeDtypeStruct((n, width), BF)
    return pl.pallas_call(
        kernel,
        name="cell_attention_backward",
        out_shape=(wide, wide, wide, jax.ShapeDtypeStruct((16, width), F32)),
        in_specs=[big] * 5 + [small] * 2,
        out_specs=(big, big, big, pl.BlockSpec(memory_space=pltpu.VMEM)),
        scratch_shapes=[
            pltpu.VMEM((2, 1536, GW), BF),
            pltpu.VMEM((2, GW, 1536), BF),
            pltpu.VMEM((512, GW), BF),
            pltpu.VMEM((512, 1024), BF),
            pltpu.VMEM((CELL, 1024), BF),
            pltpu.VMEM((CELL, 1024), BF),
            pltpu.VMEM((1024, 1024), BF),
            pltpu.VMEM((CELL, 1024), BF),
            pltpu.VMEM((512, GW), BF),
            pltpu.VMEM((4, 8, 128), jnp.int32),
            pltpu.VMEM((2, 8, 128), jnp.int32),
            pltpu.VMEM((1152, 256), F32),
            pltpu.VMEM((2, 3840, 256), BF),
            pltpu.VMEM((1152, 256), BF),
            pltpu.VMEM((4, 2, 8, 256), F32),
            pltpu.VMEM((GW, 512), BF),
            pltpu.VMEM((2, 1536, GW), F32),
            pltpu.VMEM((512, GW), BF),
            pltpu.VMEM((2, 4, CELL, GW), BF),
            pltpu.VMEM((2, 4, 2, CELL, GW), BF),
            pltpu.VMEM((2, 4, 2, CELL, GW), BF),
            pltpu.VMEM((2, 4, CELL, GW), BF),
            pltpu.VMEM((2, 4, CELL, GW), BF),
            pltpu.VMEM((4, 4, 64, GW), BF),
            pltpu.VMEM((4, 4, 64, GW), BF),
            pltpu.VMEM((4, 4, 16, GW), BF),
            pltpu.VMEM((4, 4, 16, GW), BF),
            pltpu.VMEM((4, 16, GW), BF),
            pltpu.VMEM((4, 16, 1024), BF),
            dma((8,)),
            dma((6, 4)),
            dma((6, 4)),
            dma((2, 4, 2)),
            dma((2, 4, 2)),
            dma((2, 4)),
            dma((2, 4)),
            dma((2, 4, 2)),
            dma((2, 4, 2)),
            dma((2, 4)),
            dma((2, 4)),
            dma((3, 4)),
            dma((3, 4)),
            dma((4,)),
            dma((4,)),
            dma((16,)),
            dma((16,)),
            dma((4,)),
            dma((4,)),
        ],
        compiler_params=pltpu.CompilerParams(
            collective_id=0, has_side_effects=True, vmem_limit_bytes=53 * 2**20
        ),
        cost_estimate=pl.CostEstimate(
            flops=3_000_000_000, bytes_accessed=4_000_000, transcendentals=2_000_000
        ),
    )(queries, keys, values, out_grad, out_weight, pair_counts, counts)


def solution(mesh):
    both = P(("dz", "dxy"), None)
    return jax.shard_map(
        shards,
        mesh=mesh,
        in_specs=(both, both, both, both, P(), both, P(("dz", "dxy"))),
        out_specs=(both, both, both, P("dxy", None)),
        check_vma=False,
    )
```

time: 89.6 us -> 77 us (0.86)
  the two profiles are of different devices: /device:TPU:97 before, /device:TPU:16 now
where the time goes in v2:
time: 77 us; the launch traced here: 76.9 us
  Pallas kernels  72.2 us (94%)
  local copies, waits for them, and re-layouts  3.39 us (4%)
  between operations  1.3 us (2%)
    pallas_call x1, Pallas kernels, shards(): pl.pallas_call(kernel, name='cell_attention_backward', out_shape=(wide, w...  72.2 us
    unnamed x6, local copies, waits for them, and re-layouts  3.39 us

profile of v2, /device:TPU:16, one launch (start us, length us, event | category | flops | bytes accessed | tf_op | source)
XLA Modules:
  0.0 76.9 jit_solution(3758654743885798374)
XLA Ops:
  1.3 0.0 copy-start
  1.3 0.6 copy-done
  1.9 72.2 %cell_attention_backward.1 = (bf16[128,1024]{1,0:T(8,128)(2,1)S(1)}, bf16[128,1024]{1,0:T(8,128)(2,1)S(1)}, bf16[128,1024]{1,0:T(8,128)(2,1)S(1)}, f32[16,1024]{1,0:T(8,128)S(1)}) custom-call(bf16[128,1024]{1,0:T(8,128)(2,1)} %q_hbm.1, bf16[128,1024]{1,0:T(8,128)(2,1)} %k_hbm.1, bf16[128,1024]{1,0:T(8,128)(2,1)} %v_hbm.1, bf16[128,1024]{1,0:T(8,128)(2,1)} %g_hbm.1, ...), custom_call_target="tpu_custom_call" | custom-call | flops 3000000000 | bytes 4000000 | tf_op jit(solution)/shard_map/cell_attention_backward/pallas_call | solution.py:608
  74.2 0.7 copy.16
  74.9 0.7 copy.17
  75.6 0.7 copy.18
  76.3 0.6 copy.19
Async XLA Ops:
  1.3 0.7 copy-start

commit v3 on v2

--- a/solution.py
+++ b/solution.py
@@ -11,7 +11,7 @@
 CELL = 128
 GW = 256
 DOWN, UP = 0, 1
-K_, V_, Q_, D_, G_, C_ = 0, 1, 2, 3, 4, 5
+K_, V_, Q_, G_, C_ = 0, 1, 2, 3, 4
 WAY = {(0, 0): 1, (0, 1): 2, (1, 0): 3, (1, 1): 0, (2, 0): 1, (2, 1): 2, (3, 0): 3, (3, 1): 0}
 VIA = {1: -15, 2: -3, 3: -12}
 ONTO = {1: 16, 2: 4, 3: 13}
@@ -43,12 +43,12 @@
 
 
 def kernel(
-    q_hbm, k_hbm, v_hbm, g_hbm, w_hbm, pair_ref, count_ref,
+    q_hbm, k_hbm, v_hbm, g_hbm, w_hbm, pair_hbm, count_hbm,
     dq_hbm, dk_hbm, dv_hbm, wo_ref,
-    kv, kvt, qs, gm, graw, gown, ww, dhome, do, pc, pcs,
+    kv, kvt, qs, gm, graw, gown, ww, do, pc, pcs,
     sbuf, pbuf, dsb, scale, att, acc, dqs,
     hold, back, got, hold2, fin, wsum, wgot, w2, w2got, w3, w3got,
-    loc, a_s, a_r, b_s, b_r, l_s, l_r, d_s, d_r, m_s, m_r, f_s, f_r, u_s, u_r, x_s, x_r, y_s, y_r,
+    pair_ref, count_ref, loc, a_s, a_r, b_s, b_r, l_s, l_r, d_s, d_r, m_s, m_r, f_s, f_r, u_s, u_r, x_s, x_r, y_s, y_r,
 ):
     me = lax.axis_index("dz")
     p = lax.axis_index("dxy")
@@ -118,9 +118,13 @@
         pltpu.make_async_copy(v_hbm.at[:, own], kv.at[1, rows(mine, 1)], loc.at[1]),
         pltpu.make_async_copy(q_hbm.at[:, own], qs.at[cell(mine)], loc.at[2]),
         pltpu.make_async_copy(g_hbm, graw, loc.at[3]),
-        pltpu.make_async_copy(w_hbm, ww, loc.at[4]),
+        pltpu.make_async_copy(w_hbm.at[:, own], ww, loc.at[4]),
     ]
-    for c in loads:
+    tables = [
+        pltpu.make_async_copy(pair_hbm, pair_ref, loc.at[5]),
+        pltpu.make_async_copy(count_hbm, count_ref, loc.at[6]),
+    ]
+    for c in tables + loads:
         c.start()
 
     zh, y, x = p // 16, (p // 4) % 4, p % 4
@@ -163,6 +167,8 @@
             pl.when(ok)(greet)
             expect = expect + jnp.where(ok, 1, 0)
 
+    for c in tables:
+        c.wait()
     lane = lax.broadcasted_iota(jnp.int32, (8, 128), 1)
     plain = jnp.zeros((8, 128), jnp.int32)
     turned = jnp.zeros((8, 128), jnp.int32)
@@ -190,7 +196,7 @@
             return pc.at[ll]
         if kind in (K_, V_):
             return kv.at[kind, rows(ll, 1)]
-        return {Q_: qs, D_: do, G_: gm}[kind].at[cell(ll)]
+        return {Q_: qs, G_: gm}[kind].at[cell(ll)]
 
     def spread(kind, i):
         t = group[i]
@@ -200,7 +206,7 @@
         elif kind == G_:
             src = gown
         else:
-            src = {K_: k_hbm, V_: v_hbm, Q_: q_hbm, D_: dhome}[kind].at[:, cols(t)]
+            src = {K_: k_hbm, V_: v_hbm, Q_: q_hbm}[kind].at[:, cols(t)]
         return remote(
             src, landing(kind, lt), a_s.at[kind, i], a_r.at[kind, lt], t, p
         )
@@ -209,9 +215,10 @@
         dst = landing(kind, ll)
         remote(dst, dst, a_s.at[kind, 0], a_r.at[kind, ll], sib, p).wait_recv()
 
-    for kind in (K_, V_, C_, Q_):
+    for kind in (K_, V_, C_):
         for i in range(3):
             spread(kind, i).start()
+    spread(Q_, 0).start()
 
     def halo(d, ll, kind):
         blk = kv.at[kind, rows(ll, 1)]
@@ -285,32 +292,25 @@
     send_halo(0, mine, 0)
     loads[1].wait()
     send_halo(0, mine, 1)
-    for kind in (0, 1):
-        arrived(kind, other)
-        send_halo(1, other, kind)
-
     loads[3].wait()
     live = lax.broadcasted_iota(jnp.int32, (CELL, 1024), 0) < count_ref[0]
     gown[...] = jnp.where(live, graw[...], jnp.zeros((CELL, 1024), BF))
     own_g = pltpu.make_async_copy(gown, gm.at[cell(mine)], loc.at[5])
     own_g.start()
-    spread(G_, 1).start()
     spread(G_, 0).start()
-    loads[4].wait()
-    for c in range(4):
-        dhome[:, c * GW : (c + 1) * GW] = dot(
-            gown[...], ww[:, c * GW : (c + 1) * GW]
-        ).astype(BF)
-    own_d = pltpu.make_async_copy(dhome.at[:, own], do.at[cell(mine)], loc.at[6])
-    own_d.start()
-    spread(D_, 0).start()
-
+    for kind in (0, 1):
+        arrived(kind, other)
+        send_halo(1, other, kind)
     forward_halo(0, mine)
-    forward_halo(1, other)
     for kind in (0, 1):
         for ll in (2, 3):
             arrived(kind, ll)
             send_halo(ll, ll, kind)
+        if kind == 0:
+            spread(Q_, 1).start()
+            spread(Q_, 2).start()
+            forward_halo(1, other)
+    spread(G_, 1).start()
     zl = logical(zpeer, me)
     g_fwd = remote(
         gm.at[cell(zl)], gm.at[cell(zl)], a_s.at[G_, 2], a_r.at[G_, zl], sib, p
@@ -457,14 +457,30 @@
             fin[kind, ll] = s.astype(BF)
             send_home(kind, ll, fin.at[kind, ll])
 
+    left, right = pl.ds(0, 128), pl.ds(128, 128)
+
     def stage1(e):
-        return remote(
-            wsum.at[:, (y + e) % 4], wgot.at[e], u_s.at[e], u_r.at[e], me, in_column(e)
+        return (
+            remote(
+                wsum.at[:, (y + e) % 4, :, :, left], wgot.at[0, e],
+                u_s.at[0, e], u_r.at[0, e], me, in_column(e),
+            ),
+            remote(
+                wsum.at[:, :, (x + e) % 4, :, right], wgot.at[1, e],
+                u_s.at[1, e], u_r.at[1, e], me, in_row(e),
+            ),
         )
 
     def stage2(e):
-        return remote(
-            w2.at[:, (x + e) % 4], w2got.at[e], y_s.at[e], y_r.at[e], me, in_row(e)
+        return (
+            remote(
+                w2.at[0, :, (x + e) % 4], w2got.at[0, e],
+                y_s.at[0, e], y_r.at[0, e], me, in_row(e),
+            ),
+            remote(
+                w2.at[1, :, (y + e) % 4], w2got.at[1, e],
+                y_s.at[1, e], y_r.at[1, e], me, in_column(e),
+            ),
         )
 
     def stage3(e):
@@ -475,18 +491,18 @@
         )
 
     loads[2].wait()
-    own_d.wait()
-    for kind in (C_, Q_, D_):
+    loads[4].wait()
+    own_g.wait()
+    for kind in (C_, Q_, G_):
         arrived(kind, other)
+    do[0 : 2 * CELL] = dot(gm[0 : 2 * CELL], ww[...]).astype(BF)
+    forward_halo(3, 3)
+    forward_halo(2, 2)
     halo_arrived(0)
     turn_layer(0)
     halo_arrived(1)
     turn_layer(1)
     forward(0)
-    spread(D_, 1).start()
-    spread(D_, 2).start()
-    forward_halo(2, 2)
-    forward_halo(3, 3)
     backward(0)
     send_home(2, 0, dqs.at[cell(0)])
     halo_arrived(2)
@@ -501,52 +517,59 @@
     halo_arrived(3)
     turn_layer(3)
     forward(2)
+    forward(3)
     arrived(G_, zl)
     g_fwd.start()
-    forward(3)
-    own_g.wait()
-    arrived(G_, other)
+    forward_parts(0)
     arrived(G_, 5 - zl)
     for i in range(4):
         w_t = dot(att[...], gm[:, i * 256 : (i + 1) * 256]).astype(BF)
-        wsum[i] = w_t.T.reshape(4, 64, GW)
+        wsum[i] = w_t.T.reshape(4, 4, 16, GW)
     for e in range(1, 4):
-        stage1(e).start()
-    arrived(D_, 2)
-    arrived(D_, 3)
+        for c in stage1(e):
+            c.start()
+    do[2 * CELL : 4 * CELL] = dot(gm[2 * CELL : 4 * CELL], ww[...]).astype(BF)
     backward(2)
     send_parts(1)
     send_home(2, 2, dqs.at[cell(2)])
-    forward_parts(0)
     backward(3)
+    send_parts(3)
     send_parts(2)
-    send_parts(3)
     send_home(2, 3, dqs.at[cell(3)])
+
+    s_l = wsum[:, y, :, :, 0:128].astype(F32)
+    s_r = wsum[:, :, x, :, 128:256].astype(F32)
+    for e in range(1, 4):
+        for c in stage1(e):
+            c.wait_recv()
+        s_l = s_l + wgot[0, e].astype(F32)
+        s_r = s_r + wgot[1, e].astype(F32)
+    w2[0] = s_l.astype(BF)
+    w2[1] = s_r.astype(BF)
+    for e in range(1, 4):
+        for c in stage2(e):
+            c.start()
     finish(0)
-
-    s1 = wsum[:, y].astype(F32)
+    forward_parts(1)
+
+    s_l = w2[0, :, x].astype(F32)
+    s_r = w2[1, :, y].astype(F32)
     for e in range(1, 4):
-        stage1(e).wait_recv()
-        s1 = s1 + wgot[e].astype(F32)
-    w2[...] = s1.astype(BF).reshape(4, 4, 16, GW)
-    for e in range(1, 4):
-        stage2(e).start()
-    forward_parts(1)
-    finish(1)
-    forward_parts(2)
-
-    s2 = w2[:, x].astype(F32)
-    for e in range(1, 4):
-        stage2(e).wait_recv()
-        s2 = s2 + w2got[e].astype(F32)
-    w3[...] = s2.astype(BF)
+        for c in stage2(e):
+            c.wait_recv()
+        s_l = s_l + w2got[0, e].astype(F32)
+        s_r = s_r + w2got[1, e].astype(F32)
+    w3[:, :, 0:128] = s_l.astype(BF)
+    w3[:, :, 128:256] = s_r.astype(BF)
     for e in range(1, 16):
         stage3(e).start()
     own_x = pltpu.make_async_copy(w3.at[zh], w3got.at[zh, :, cols(me)], loc.at[7])
     own_x.start()
+    finish(1)
     forward_parts(3)
+    forward_parts(2)
+    finish(3)
     finish(2)
-    finish(3)
     own_x.wait()
     for e in range(1, 16):
         came = (at - e + 16) % 16
@@ -565,15 +588,15 @@
         sent_home(0, ll, fin.at[0, ll])
         sent_home(1, ll, fin.at[1, ll])
         sent_home(2, ll, dqs.at[cell(ll)])
-    for kind in (K_, V_, Q_, D_, C_):
+    for kind in (K_, V_, Q_, C_):
         for i in range(3):
             spread(kind, i).wait_send()
     spread(G_, 0).wait_send()
     spread(G_, 1).wait_send()
     g_fwd.wait_send()
     for e in range(1, 4):
-        stage1(e).wait_send()
-        stage2(e).wait_send()
+        for c in stage1(e) + stage2(e):
+            c.wait_send()
     for e in range(1, 16):
         stage3(e).wait_send()
     for d in (UP, DOWN):
@@ -602,14 +625,13 @@
 def shards(queries, keys, values, out_grad, out_weight, pair_counts, counts):
     n, width = queries.shape
     big = pl.BlockSpec(memory_space=pltpu.HBM)
-    small = pl.BlockSpec(memory_space=pltpu.SMEM)
     dma = pltpu.SemaphoreType.DMA
     wide = jax.ShapeDtypeStruct((n, width), BF)
     return pl.pallas_call(
         kernel,
         name="cell_attention_backward",
         out_shape=(wide, wide, wide, jax.ShapeDtypeStruct((16, width), F32)),
-        in_specs=[big] * 5 + [small] * 2,
+        in_specs=[big] * 7,
         out_specs=(big, big, big, pl.BlockSpec(memory_space=pltpu.VMEM)),
         scratch_shapes=[
             pltpu.VMEM((2, 1536, GW), BF),
@@ -618,8 +640,7 @@
             pltpu.VMEM((512, 1024), BF),
             pltpu.VMEM((CELL, 1024), BF),
             pltpu.VMEM((CELL, 1024), BF),
-            pltpu.VMEM((1024, 1024), BF),
-            pltpu.VMEM((CELL, 1024), BF),
+            pltpu.VMEM((1024, GW), BF),
             pltpu.VMEM((512, GW), BF),
             pltpu.VMEM((4, 8, 128), jnp.int32),
             pltpu.VMEM((2, 8, 128), jnp.int32),
@@ -635,15 +656,17 @@
             pltpu.VMEM((2, 4, 2, CELL, GW), BF),
             pltpu.VMEM((2, 4, CELL, GW), BF),
             pltpu.VMEM((2, 4, CELL, GW), BF),
-            pltpu.VMEM((4, 4, 64, GW), BF),
-            pltpu.VMEM((4, 4, 64, GW), BF),
-            pltpu.VMEM((4, 4, 16, GW), BF),
-            pltpu.VMEM((4, 4, 16, GW), BF),
+            pltpu.VMEM((4, 4, 4, 16, GW), BF),
+            pltpu.VMEM((2, 4, 4, 4, 16, 128), BF),
+            pltpu.VMEM((2, 4, 4, 16, 128), BF),
+            pltpu.VMEM((2, 4, 4, 16, 128), BF),
             pltpu.VMEM((4, 16, GW), BF),
             pltpu.VMEM((4, 16, 1024), BF),
+            pltpu.SMEM((1, 9), jnp.int32),
+            pltpu.SMEM((1,), jnp.int32),
             dma((8,)),
-            dma((6, 4)),
-            dma((6, 4)),
+            dma((5, 4)),
+            dma((5, 4)),
             dma((2, 4, 2)),
             dma((2, 4, 2)),
             dma((2, 4)),
@@ -654,12 +677,12 @@
             dma((2, 4)),
             dma((3, 4)),
             dma((3, 4)),
-            dma((4,)),
-            dma((4,)),
+            dma((2, 4)),
+            dma((2, 4)),
             dma((16,)),
             dma((16,)),
-            dma((4,)),
-            dma((4,)),
+            dma((2, 4)),
+            dma((2, 4)),
         ],
         compiler_params=pltpu.CompilerParams(
             collective_id=0, has_side_effects=True, vmem_limit_bytes=53 * 2**20

time: 77 us -> 73.2 us (0.951)
  the two profiles are of different devices: /device:TPU:16 before, /device:TPU:31 now
where the time goes in v3:
time: 73.2 us; the launch traced here: 73.1 us
  Pallas kernels  68.4 us (93%)
  local copies, waits for them, and re-layouts  3.39 us (5%)
  between operations  1.3 us (2%)
    pallas_call x1, Pallas kernels, shards(): pl.pallas_call(kernel, name='cell_attention_backward', out_shape=(wide, w...  68.4 us
    unnamed x6, local copies, waits for them, and re-layouts  3.39 us

profile of v3, /device:TPU:31, one launch (start us, length us, event | category | flops | bytes accessed | tf_op | source)
XLA Modules:
  0.0 73.1 jit_solution(1911068157468416891)
XLA Ops:
  1.3 0.0 copy-start
  1.3 0.6 copy-done
  1.9 68.4 %cell_attention_backward.1 = (bf16[128,1024]{1,0:T(8,128)(2,1)S(1)}, bf16[128,1024]{1,0:T(8,128)(2,1)S(1)}, bf16[128,1024]{1,0:T(8,128)(2,1)S(1)}, f32[16,1024]{1,0:T(8,128)S(1)}) custom-call(bf16[128,1024]{1,0:T(8,128)(2,1)} %q_hbm.1, bf16[128,1024]{1,0:T(8,128)(2,1)} %k_hbm.1, bf16[128,1024]{1,0:T(8,128)(2,1)} %v_hbm.1, bf16[128,1024]{1,0:T(8,128)(2,1)} %g_hbm.1, ...), custom_call_target="tpu_custom_call" | custom-call | flops 3000000000 | bytes 4000000 | tf_op jit(solution)/shard_map/cell_attention_backward/pallas_call | solution.py:630
  70.4 0.7 copy.16
  71.1 0.7 copy.17
  71.8 0.7 copy.18
  72.5 0.6 copy.19
Async XLA Ops:
  1.3 0.7 copy-start

commit v4 on v3

--- a/solution.py
+++ b/solution.py
@@ -549,8 +549,9 @@
     for e in range(1, 4):
         for c in stage2(e):
             c.start()
+    forward_parts(1)
+    forward_parts(3)
     finish(0)
-    forward_parts(1)
 
     s_l = w2[0, :, x].astype(F32)
     s_r = w2[1, :, y].astype(F32)
@@ -565,9 +566,8 @@
         stage3(e).start()
     own_x = pltpu.make_async_copy(w3.at[zh], w3got.at[zh, :, cols(me)], loc.at[7])
     own_x.start()
+    forward_parts(2)
     finish(1)
-    forward_parts(3)
-    forward_parts(2)
     finish(3)
     finish(2)
     own_x.wait()

time: 73.2 us -> 72.6 us (level)
  no operation moved by 1% of the time
where the time goes in v4:
time: 72.6 us; the launch traced here: 72.5 us
  Pallas kernels  67.8 us (93%)
  local copies, waits for them, and re-layouts  3.39 us (5%)
  between operations  1.3 us (2%)
    pallas_call x1, Pallas kernels, shards(): pl.pallas_call(kernel, name='cell_attention_backward', out_shape=(wide, w...  67.8 us
    unnamed x6, local copies, waits for them, and re-layouts  3.39 us

profile of v4, /device:TPU:31, one launch (start us, length us, event | category | flops | bytes accessed | tf_op | source)
XLA Modules:
  0.0 72.5 jit_solution(2630286213878305868)
XLA Ops:
  1.3 0.0 copy-start
  1.3 0.6 copy-done
  1.9 67.8 %cell_attention_backward.1 = (bf16[128,1024]{1,0:T(8,128)(2,1)S(1)}, bf16[128,1024]{1,0:T(8,128)(2,1)S(1)}, bf16[128,1024]{1,0:T(8,128)(2,1)S(1)}, f32[16,1024]{1,0:T(8,128)S(1)}) custom-call(bf16[128,1024]{1,0:T(8,128)(2,1)} %q_hbm.1, bf16[128,1024]{1,0:T(8,128)(2,1)} %k_hbm.1, bf16[128,1024]{1,0:T(8,128)(2,1)} %v_hbm.1, bf16[128,1024]{1,0:T(8,128)(2,1)} %g_hbm.1, ...), custom_call_target="tpu_custom_call" | custom-call | flops 3000000000 | bytes 4000000 | tf_op jit(solution)/shard_map/cell_attention_backward/pallas_call | solution.py:630
  69.8 0.7 copy.16
  70.5 0.7 copy.17
  71.2 0.7 copy.18
  71.9 0.6 copy.19
Async XLA Ops:
  1.3 0.7 copy-start

commit v5 on v4

--- a/solution.py
+++ b/solution.py
@@ -517,9 +517,9 @@
     halo_arrived(3)
     turn_layer(3)
     forward(2)
-    forward(3)
     arrived(G_, zl)
     g_fwd.start()
+    forward(3)
     forward_parts(0)
     arrived(G_, 5 - zl)
     for i in range(4):

time: 72.6 us -> 72.2 us (level)
  no operation moved by 1% of the time
where the time goes in v5:
time: 72.2 us; the launch traced here: 72.1 us
  Pallas kernels  67.5 us (93%)
  local copies, waits for them, and re-layouts  3.39 us (5%)
  between operations  1.3 us (2%)
    pallas_call x1, Pallas kernels, shards(): pl.pallas_call(kernel, name='cell_attention_backward', out_shape=(wide, w...  67.5 us
    unnamed x6, local copies, waits for them, and re-layouts  3.39 us

profile of v5, /device:TPU:31, one launch (start us, length us, event | category | flops | bytes accessed | tf_op | source)
XLA Modules:
  0.0 72.1 jit_solution(9731596149273544627)
XLA Ops:
  1.3 0.0 copy-start
  1.3 0.6 copy-done
  1.9 67.5 %cell_attention_backward.1 = (bf16[128,1024]{1,0:T(8,128)(2,1)S(1)}, bf16[128,1024]{1,0:T(8,128)(2,1)S(1)}, bf16[128,1024]{1,0:T(8,128)(2,1)S(1)}, f32[16,1024]{1,0:T(8,128)S(1)}) custom-call(bf16[128,1024]{1,0:T(8,128)(2,1)} %q_hbm.1, bf16[128,1024]{1,0:T(8,128)(2,1)} %k_hbm.1, bf16[128,1024]{1,0:T(8,128)(2,1)} %v_hbm.1, bf16[128,1024]{1,0:T(8,128)(2,1)} %g_hbm.1, ...), custom_call_target="tpu_custom_call" | custom-call | flops 3000000000 | bytes 4000000 | tf_op jit(solution)/shard_map/cell_attention_backward/pallas_call | solution.py:630
  69.4 0.7 copy.16
  70.1 0.7 copy.17
  70.8 0.7 copy.18
  71.5 0.6 copy.19
Async XLA Ops:
  1.3 0.7 copy-start
